TPU v7x, 32 devices: a whole 2x2x4 slice. The times are simulated.
32 devices in a mesh: batch: 16 (over z, y, core), blk: 2 (over x).
Axes of the slice: x: 2, y: 2, z: 4, core: 2. Of those that a mesh axis runs over, the one named last changes fastest.
Arguments:
- tokens: bfloat16 [16, 2, 1024, 768], P('batch', None, 'blk'), may hold values from -6 to 6
- cotangent: bfloat16 [16, 2, 1024, 768], P('batch', None, 'blk'), may hold values from -6 to 6
- counts: int32 [16], P('batch'), may hold values from 2 to 3
- perms: int32 [2, 12, 3], replicated, may hold values from 0 to 2, as said below
- key_mask: int32 [16, 2, 1024], P('batch', None, 'blk'), may hold values from 0 to 1, as said below
- w_qkv: bfloat16 [768, 2304], replicated, may hold values from -0.21875 to 0.21875
- bias_q: float32 [768], replicated, may hold values from -3 to 3
- bias_v: float32 [768], replicated, may hold values from -3 to 3
- w_out: bfloat16 [768, 768], replicated, may hold values from -0.875 to 0.875
- bias_out: float32 [768], replicated, may hold values from -3 to 3
- gain_one: float32 [768], replicated, may hold values from 0.5 to 1.5
- shift_one: float32 [768], replicated, may hold values from -3 to 3
- w_in: bfloat16 [768, 3072], replicated, may hold values from -0.21875 to 0.21875
- bias_in: float32 [3072], replicated, may hold values from -3 to 3
- w_back: bfloat16 [3072, 768], replicated, may hold values from -0.109375 to 0.109375
- bias_back: float32 [768], replicated, may hold values from -3 to 3
- gain_two: float32 [768], replicated, may hold values from 0.5 to 1.5
- shift_two: float32 [768], replicated, may hold values from -3 to 3
Outputs:
- mixed_out: bfloat16 [16, 2, 1024, 768], P('batch', None, 'blk')
- tokens_grad: bfloat16 [16, 2, 1024, 768], P('batch', None, 'blk')
- w_qkv_grad: float32 [768, 2304], P('batch')
- bias_q_grad: float32 [768], P('batch')
- bias_v_grad: float32 [768], P('batch')
- w_out_grad: float32 [768, 768], P('batch')
- bias_out_grad: float32 [768], P('batch')
- gain_one_grad: float32 [768], P('batch')
- shift_one_grad: float32 [768], P('batch')
- w_in_grad: float32 [768, 3072], P('batch')
- bias_in_grad: float32 [3072], P('batch')
- w_back_grad: float32 [3072, 768], P('batch')
- bias_back_grad: float32 [768], P('batch')
- gain_two_grad: float32 [768], P('batch')
- shift_two_grad: float32 [768], P('batch')
Inputs may be any that keep to these rules, and one draw needn't show every extreme that they name: `perms`: row 0 holds for each head a permutation of 0 and 1 followed by 2; row 1 holds for each head a permutation of 0, 1, 2. `key_mask`: the first token of every block of 512 tokens is 1.
All inputs are finite; a program needn't handle non-finite values.
Results may differ from a plain program's by a relative error of at most 0.014.
Values may be sent and summed in bfloat16 or wider, within the bound.
No kernel may reach another device: no remote copies, remote signals or barrier semaphores. Data moves between devices by JAX's collectives and lax.ppermute only.
A program may use at most 192 MiB of HBM per device.

v0:
```python
import jax
import jax.numpy as jnp
from jax import lax
from jax.sharding import PartitionSpec as P

EPSILON = 1e-05
HIGHEST = lax.Precision.HIGHEST


def from_partner(block, axis, apart):
    count = lax.axis_size(axis)
    route = []
    for low in range(count):
        high = low | 1 << apart
        if high != low and high < count:
            route += [(low, high), (high, low)]
    return lax.ppermute(block, axis, route)


def layer_norm(hidden, norm_gain, norm_shift):
    centre = jnp.mean(hidden, axis=-1, keepdims=True)
    centred = hidden - centre
    spread = jnp.mean(centred * centred, axis=-1, keepdims=True)
    return centred * lax.rsqrt(spread + EPSILON) * norm_gain + norm_shift


def exact_gelu(hidden):
    return jax.nn.gelu(hidden, approximate=False)


def contract_rows(left_side, right_side):
    return lax.dot_general(
        left_side, right_side, (((0,), (0,)), ((), ())), preferred_element_type=jnp.float32
    )


def contract_cols(left_side, right_side):
    return lax.dot_general(
        left_side, right_side, (((1,), (1,)), ((), ())), preferred_element_type=jnp.float32
    )


def place_sides(own_part, other_part, my_side):
    lower_side = jnp.where(my_side == 0, own_part, other_part)
    upper_side = jnp.where(my_side == 0, other_part, own_part)
    return jnp.stack([lower_side, upper_side], axis=2)


def split_sides(paired, my_side):
    lower_side = paired[:, :, 0]
    upper_side = paired[:, :, 1]
    own_part = jnp.where(my_side == 0, lower_side, upper_side)
    other_part = jnp.where(my_side == 0, upper_side, lower_side)
    return (own_part, other_part)


def masked_scores(queries, keys_used, mask_used):
    scores = (
        jnp.einsum("sqhe,skhe->shqk", queries, keys_used, preferred_element_type=jnp.float32)
        * 0.125
    )
    return jnp.where(mask_used[:, :, None, :] > 0.5, scores, -1e30)


def attend_forward(pieces):
    queries, keys_used, values_used, mask_used = pieces
    scores = masked_scores(queries, keys_used, mask_used)
    highest = jnp.max(scores, axis=-1, keepdims=True)
    weights = jnp.exp(scores - highest)
    totals = jnp.sum(weights, axis=-1, keepdims=True)
    probs_low = (weights / totals).astype(jnp.bfloat16)
    attended = jnp.einsum(
        "shqk,skhe->sqhe", probs_low, values_used, preferred_element_type=jnp.float32
    )
    return (attended.astype(jnp.bfloat16), highest + jnp.log(totals))


def attend_backward(pieces):
    queries, keys_used, values_used, mask_used, log_totals, grad_out = pieces
    scores = masked_scores(queries, keys_used, mask_used)
    probs_full = jnp.exp(scores - log_totals)
    probs_low = probs_full.astype(jnp.bfloat16)
    grad_values = jnp.einsum(
        "shqk,sqhe->skhe", probs_low, grad_out, preferred_element_type=jnp.float32
    )
    grad_probs = jnp.einsum(
        "sqhe,skhe->shqk", grad_out, values_used, preferred_element_type=jnp.float32
    )
    row_dot = jnp.sum(probs_full * grad_probs, axis=-1, keepdims=True)
    grad_scores = (probs_full * (grad_probs - row_dot)).astype(jnp.bfloat16)
    grad_queries = (
        jnp.einsum("shqk,skhe->sqhe", grad_scores, keys_used, preferred_element_type=jnp.float32)
        * 0.125
    )
    grad_keys = (
        jnp.einsum("shqk,sqhe->skhe", grad_scores, queries, preferred_element_type=jnp.float32)
        * 0.125
    )
    return (grad_queries, grad_keys, grad_values)


def local(
    tokens,
    cotangent,
    counts,
    perms,
    key_mask,
    w_qkv,
    bias_q,
    bias_v,
    w_out,
    bias_out,
    gain_one,
    shift_one,
    w_in,
    bias_in,
    w_back,
    bias_back,
    gain_two,
    shift_two,
):
    item_count, slot_count, block_rows, model_width = tokens.shape
    head_count = perms.shape[1]
    head_width = model_width // head_count
    my_side = lax.axis_index("blk")
    token_rows = tokens.reshape(-1, model_width)
    slab_shape = (item_count, slot_count, block_rows, model_width)
    projected = jnp.dot(token_rows, w_qkv, preferred_element_type=jnp.float32)
    queries = (projected[:, :model_width] + bias_q).astype(jnp.bfloat16)
    keys_own = projected[:, model_width : 2 * model_width].astype(jnp.bfloat16).reshape(slab_shape)
    values_own = (projected[:, 2 * model_width :] + bias_v).astype(jnp.bfloat16).reshape(slab_shape)
    mask_own = key_mask.astype(jnp.bfloat16)
    partner_keys, partner_values, partner_mask = from_partner(
        (keys_own, values_own, mask_own), "blk", 0
    )
    lookup = jnp.where((counts == 2)[:, None, None], perms[0][None], perms[1][None])
    extended = jnp.concatenate(
        [lookup, jnp.full((item_count, head_count, 1), 3, jnp.int32)], axis=2
    )
    local_blocks = 2 * jnp.arange(slot_count, dtype=jnp.int32) + my_side
    picked = jnp.take(extended, local_blocks, axis=2)
    sources = jnp.where(
        local_blocks[None, None, :] < counts[:, None, None], picked, local_blocks[None, None, :]
    )
    choose = (sources[..., None] == jnp.arange(4, dtype=jnp.int32)).astype(jnp.float32)
    choose_low = choose.astype(jnp.bfloat16)
    live_blocks = (local_blocks[None, :] < counts[:, None]).astype(jnp.float32)
    live_rows = jnp.broadcast_to(
        live_blocks[:, :, None], (item_count, slot_count, block_rows)
    ).reshape(-1)
    head_shape = (item_count, 4, block_rows, head_count, head_width)
    keys_all = place_sides(keys_own, partner_keys, my_side).reshape(head_shape)
    values_all = place_sides(values_own, partner_values, my_side).reshape(head_shape)
    mask_all = (
        place_sides(mask_own, partner_mask, my_side)
        .reshape(item_count, 4, block_rows)
        .astype(jnp.float32)
    )
    keys_used = jnp.einsum(
        "ihsc,icthe->isthe", choose_low, keys_all, preferred_element_type=jnp.float32
    ).astype(jnp.bfloat16)
    values_used = jnp.einsum(
        "ihsc,icthe->isthe", choose_low, values_all, preferred_element_type=jnp.float32
    ).astype(jnp.bfloat16)
    mask_used = jnp.einsum("ihsc,ict->isht", choose, mask_all, precision=HIGHEST)
    query_heads = queries.reshape(item_count, slot_count, block_rows, head_count, head_width)
    attended, log_totals = lax.map(attend_forward, (query_heads, keys_used, values_used, mask_used))
    attended_rows = attended.reshape(-1, model_width)
    first_sum = (
        token_rows.astype(jnp.float32)
        + jnp.dot(attended_rows, w_out, preferred_element_type=jnp.float32)
        + bias_out
    )
    normed, first_pull = jax.vjp(layer_norm, first_sum, gain_one, shift_one)
    normed_low = normed.astype(jnp.bfloat16)
    hidden_pre = jnp.dot(normed_low, w_in, preferred_element_type=jnp.float32) + bias_in
    active_full, gelu_pull = jax.vjp(exact_gelu, hidden_pre)
    active = active_full.astype(jnp.bfloat16)
    second = normed + jnp.dot(active, w_back, preferred_element_type=jnp.float32) + bias_back
    result_two, second_pull = jax.vjp(layer_norm, second, gain_two, shift_two)
    mixed_out = (result_two * live_rows[:, None]).astype(jnp.bfloat16).reshape(slab_shape)
    cot_rows = cotangent.reshape(-1, model_width).astype(jnp.float32) * live_rows[:, None]
    grad_second, grad_gain_two, grad_shift_two = second_pull(cot_rows)
    grad_bias_back = jnp.sum(grad_second, axis=0)
    back_low = grad_second.astype(jnp.bfloat16)
    grad_w_back = contract_rows(active, back_low)
    grad_active = contract_cols(back_low, w_back)
    (grad_hidden,) = gelu_pull(grad_active)
    grad_bias_in = jnp.sum(grad_hidden, axis=0)
    hidden_low = grad_hidden.astype(jnp.bfloat16)
    grad_w_in = contract_rows(normed_low, hidden_low)
    grad_normed = grad_second + contract_cols(hidden_low, w_in)
    grad_first, grad_gain_one, grad_shift_one = first_pull(grad_normed)
    grad_bias_out = jnp.sum(grad_first, axis=0)
    first_low = grad_first.astype(jnp.bfloat16)
    grad_w_out = contract_rows(attended_rows, first_low)
    grad_attended = (
        contract_cols(first_low, w_out)
        .astype(jnp.bfloat16)
        .reshape(item_count, slot_count, block_rows, head_count, head_width)
    )
    grad_queries, grad_keys_used, grad_values_used = lax.map(
        attend_backward, (query_heads, keys_used, values_used, mask_used, log_totals, grad_attended)
    )
    side_shape = (item_count, 2, 2, block_rows, model_width)
    keys_back = jnp.einsum("ihsc,isthe->icthe", choose, grad_keys_used, precision=HIGHEST).reshape(
        side_shape
    )
    values_back = jnp.einsum(
        "ihsc,isthe->icthe", choose, grad_values_used, precision=HIGHEST
    ).reshape(side_shape)
    own_keys, other_keys = split_sides(keys_back, my_side)
    own_values, other_values = split_sides(values_back, my_side)
    came_keys, came_values = (
        from_partner(other_keys.astype(jnp.bfloat16), "blk", 0).astype(other_keys.dtype),
        from_partner(other_values.astype(jnp.bfloat16), "blk", 0).astype(other_values.dtype),
    )
    grad_keys = (own_keys + came_keys).reshape(-1, model_width)
    grad_values = (own_values + came_values).reshape(-1, model_width)
    grad_query_rows = grad_queries.reshape(-1, model_width)
    grad_bias_q = jnp.sum(grad_query_rows, axis=0)
    grad_bias_v = jnp.sum(grad_values, axis=0)
    projected_low = jnp.concatenate([grad_query_rows, grad_keys, grad_values], axis=1).astype(
        jnp.bfloat16
    )
    grad_w_qkv = contract_rows(token_rows, projected_low)
    tokens_grad = (
        (grad_first + contract_cols(projected_low, w_qkv)).astype(jnp.bfloat16).reshape(slab_shape)
    )
    gradients = (
        grad_w_qkv,
        grad_bias_q,
        grad_bias_v,
        grad_w_out,
        grad_bias_out,
        grad_gain_one,
        grad_shift_one,
        grad_w_in,
        grad_bias_in,
        grad_w_back,
        grad_bias_back,
        grad_gain_two,
        grad_shift_two,
    )
    batch_count = lax.axis_size("batch")
    pair_count = lax.axis_size("blk")
    by_owner = jnp.concatenate(
        [gradient.reshape(batch_count, -1) for gradient in gradients], axis=1
    )
    span_width = by_owner.shape[1]
    spread_rows = by_owner.reshape(batch_count * pair_count, span_width // pair_count)
    shares = lax.psum_scatter(spread_rows, ("batch", "blk"), scatter_dimension=0, tiled=True)
    summed = (
        lax.all_gather(shares.astype(jnp.bfloat16), "blk", axis=0, tiled=True)
        .astype(shares.dtype)
        .reshape(-1)
    )
    results = [mixed_out, tokens_grad]
    offset = 0
    for gradient in gradients:
        piece_size = gradient.size // batch_count
        piece_shape = (gradient.shape[0] // batch_count,) + gradient.shape[1:]
        results.append(summed[offset : offset + piece_size].reshape(piece_shape))
        offset = offset + piece_size
    return tuple(results)


def solution(mesh):
    in_specs = (
        P("batch", None, "blk", None),
        P("batch", None, "blk", None),
        P("batch"),
        P(),
        P("batch", None, "blk"),
        P(),
        P(),
        P(),
        P(),
        P(),
        P(),
        P(),
        P(),
        P(),
        P(),
        P(),
        P(),
        P(),
    )
    out_specs = (
        P("batch", None, "blk", None),
        P("batch", None, "blk", None),
        P("batch", None),
        P("batch"),
        P("batch"),
        P("batch", None),
        P("batch"),
        P("batch"),
        P("batch"),
        P("batch", None),
        P("batch"),
        P("batch", None),
        P("batch"),
        P("batch"),
        P("batch"),
    )
    return jax.shard_map(local, mesh=mesh, in_specs=in_specs, out_specs=out_specs, check_vma=False)
```

profile of v0, /device:TPU:0, one launch (start us, length us, event | category | flops | bytes accessed | tf_op | source)
XLA Modules:
  0.0 1164.8 jit_solution(13721421052255676325)
XLA Ops:
  2.7 5.3 fusion.92
  31.8 49.9 %collective-permute-done.1 = bf16[1,2,512]{2,1,0:T(2,128)(2,1)} collective-permute-done((bf16[1,2,512]{2,1,0:T(2,128)(2,1)}, bf16[1,2,512]{2,1,0:T(2,128)(2,1)}, u32[]{:S(2)}, u32[]{:S(2)}) %collective-permute-start.1) | collective-permute-done | bytes 2080 | tf_op jit(solution)/shard_map/ppermute | solution.py:17
  83.8 4.9 select_bitcast_fusion.1
  90.7 8.8 copy.83
  99.5 8.1 reshape.505
  107.6 5.0 fusion.42
  114.5 8.8 copy.78
  123.3 8.1 reshape.502
  131.4 4.8 fusion.41
  136.2 6.7 fusion.12
  142.9 5.9 fusion
  151.2 9.1 fusion.43
  168.4 35.2 %multiply_convert_fusion.1 = (bf16[1024,3072]{1,0:T(8,128)(2,1)S(1)}, f32[1024,3072]{1,0:T(8,128)}, f32[1024,3072]{1,0:T(8,128)}) fusion(f32[3072]{0:T(1024)S(1)} %copy-done.48, bf16[768,3072]{1,0:T(8,128)(2,1)S(1)} %bitcast.165, f32[1024,768]{1,0:T(8,128)S(1)} %get-tuple-element.107, f32[768]{0:T(1024)S(1)} %copy-done.29, f32[768]{0:T(1024)S(1)} %copy-done.26, ...), kind=kOutput, calls=%fused_computation.14 | convolution fusion | flops 5043388416 | bytes 39348224 | tf_op jit(solution)/shard_map/dot_general | solution.py:176
  203.7 5.4 fusion.90
  216.7 17.5 %fusion.91 = (f32[3072]{0:T(1024)}, bf16[1024,3072]{1,0:T(8,128)(2,1)}) fusion(f32[1024,3072]{1,0:T(8,128)} %get-tuple-element.78, bf16[3072,768]{1,0:T(8,128)(2,1)} %param.32, f32[1024,768]{1,0:T(8,128)} %get-tuple-element.74, f32[1024]{0:T(1024)} %negate_multiply_fusion.2, f32[1024,3072]{1,0:T(8,128)} %get-tuple-element.108, f32[3072]{0:T(1024)} %param.31), kind=kOutput, calls=%fused_computation.163 | convolution fusion | flops 4883739648 | bytes 39350272 | tf_op jit(solution)/shard_map/dot_general | solution.py:38
  234.2 11.7 %multiply_reduce_fusion.3 = (f32[768]{0:T(1024)}, f32[1024]{0:T(1024)S(1)}, f32[768]{0:T(1024)}, f32[1024,768]{1,0:T(8,128)S(1)}) fusion(f32[1024,768]{1,0:T(8,128)} %copy-done.3, f32[1024]{0:T(1024)S(1)} %fusion.63, f32[1024]{0:T(1024)S(1)} %broadcast_multiply_fusion.1, f32[768]{0:T(1024)S(1)} %copy-done.26, bf16[768,3072]{1,0:T(8,128)(2,1)} %param.30, ...), kind=kOutput, calls=%fused_computation.53 | convolution fusion | flops 4839699456 | bytes 20472832 | tf_op jit(solution)/shard_map/dot_general | solution.py:38
  258.2 23.0 %multiply_reduce_fusion = (f32[2,12,512]{2,1,0:T(8,128)S(1)}, f32[2,12,512,512]{2,3,1,0:T(8,128)}) fusion(f32[2,12,512]{2,1,0:T(8,128)} %log_add_fusion, f32[2,12,512,512]{2,3,1,0:T(8,128)} %copy-done.1, pred[2,12,512]{2,1,0:T(8,128)(4,1)S(1)} %copy-done.20, bf16[2,512,12,64]{1,0,3,2:T(2,128)(2,1)} %fusion.41, bf16[2,512,12,64]{1,0,3,2:T(2,128)(2,1)} %squeeze.38), kind=kOutput, calls=%fused_computation.2 | convolution fusion | flops 836751360 | bytes 53587968 | tf_op jit(solution)/shard_map/while/body/eval_jaxpr/sqhe,skhe->shqk/dot_general | solution.py:86
  281.3 17.3 %multiply_convert_fusion = bf16[2,12,512,512]{2,3,1,0:T(8,128)(2,1)S(1)} fusion(f32[2,12,512,512]{2,3,1,0:T(8,128)} %get-tuple-element.113, f32[2,12,512]{2,1,0:T(8,128)S(1)} %get-tuple-element.112, f32[2,12,512]{2,1,0:T(8,128)S(1)} %copy-done.18, f32[2,12,512,512]{2,3,1,0:T(8,128)} %copy-done.1, pred[2,12,512]{2,1,0:T(8,128)(4,1)S(1)} %copy-done.20), kind=kLoop, calls=%fused_computation.1 | loop fusion | flops 37748736 | bytes 63025152 | tf_op jit(solution)/shard_map/while/body/eval_jaxpr/convert_element_type | solution.py:90
  306.9 8.6 multiply_bitcast_fusion
  315.6 13.1 %fusion.33 = f32[2,512,12,64]{1,3,2,0:T(8,128)} fusion(f32[2,12,512]{2,1,0:T(8,128)S(1)} %copy-done.18, f32[2,12,512,512]{2,3,1,0:T(8,128)} %copy-done.1, pred[2,12,512]{2,1,0:T(8,128)(4,1)S(1)} %copy-done.20, bf16[2,512,12,64]{1,0,3,2:T(2,128)(2,1)S(1)} %copy-done.14), kind=kOutput, calls=%fused_computation.80 | convolution fusion | flops 830472192 | bytes 29945856 | tf_op jit(solution)/shard_map/while/body/eval_jaxpr/shqk,sqhe->skhe/dot_general | solution.py:83
  328.7 10.8 fusion.20
  339.5 10.9 fusion.76
  353.6 8.9 fusion.25
  362.5 8.9 reshape.509
  371.4 12.8 %fusion.85 = (f32[1,2,1,512,768]{3,2,1,4,0:T(1,128)}, f32[1,2,1,512,768]{3,2,1,4,0:T(1,128)}) fusion(f32[1,2,2,512,768]{3,2,1,4,0:T(2,128)} %reshape.509), kind=kLoop, calls=%fused_computation.157 | loop fusion | bytes 12582912 | tf_op jit(solution)/shard_map/slice | solution.py:50
  384.2 8.5 copy.116
  392.7 8.5 copy.117
  406.5 9.1 fusion.28
  415.6 8.9 reshape.511
  424.5 12.7 %fusion.86 = (f32[1,2,1,512,768]{3,2,1,4,0:T(1,128)}, f32[1,2,1,512,768]{3,2,1,4,0:T(1,128)}) fusion(f32[1,2,2,512,768]{3,2,1,4,0:T(2,128)} %reshape.511), kind=kLoop, calls=%fused_computation.158 | loop fusion | bytes 12582912 | tf_op jit(solution)/shard_map/slice | solution.py:50
  437.2 8.5 copy.118
  445.7 8.7 copy.119
  459.2 5.2 fusion.77
  471.6 10.7 reshape.521
  483.1 10.7 reshape.523
  505.9 4.7 fusion.57
  513.1 9.5 convolution_bitcast_fusion
  522.7 8.0 copy.107
  530.7 5.6 reshape.514
  536.2 6.3 constant_dynamic-update-slice_fusion
  546.7 8.2 dynamic-update-slice.3
  559.4 27.4 %dynamic-update-slice.7 = f32[16,442944]{1,0:T(8,128)} dynamic-update-slice(f32[16,442944]{1,0:T(8,128)} %dynamic-update-slice.6, f32[16,147456]{1,0:T(8,128)} %reshape.521, s32[]{} %constant.167, s32[]{} %constant.174) | dynamic-update-slice | bytes 18874372
  588.3 27.0 %dynamic-update-slice.9 = f32[16,442944]{1,0:T(8,128)} dynamic-update-slice(f32[16,442944]{1,0:T(8,128)} %dynamic-update-slice.8, f32[16,147456]{1,0:T(8,128)} %reshape.523, s32[]{} %constant.167, s32[]{} %constant.176) | dynamic-update-slice | bytes 18874372
  619.6 28.2 %reshape.527 = f32[32,221472]{1,0:T(8,128)} reshape(f32[16,442944]{1,0:T(8,128)} %dynamic-update-slice.12) | data formatting | bytes 56696832 | tf_op jit(solution)/shard_map/reshape | solution.py:251
  647.8 456.4 %all-reduce.3 = bf16[32,221472]{1,0:T(8,128)(2,1)} all-reduce(f32[32,221472]{1,0:T(8,128)} %reshape.527), channel_id=2, replica_groups=mesh['batch'=16,'blk'=2] {'batch','blk'}, use_global_device_ids=true, to_apply=%region_20.21.clone | all-reduce | flops 7087104 | bytes 42522624
  1106.7 22.0 %all-gather = bf16[2,1,221472]{2,1,0:T(2,128)(2,1)S(1)} all-gather(bf16[1,1,221472]{2,1,0:T(2,128)(2,1)S(1)} %fusion.56), channel_id=1, replica_groups=mesh['batch'=16,'blk'=2] {'blk'}, dimensions={0}, use_global_device_ids=true | all-gather | bytes 1328832 | tf_op jit(solution)/shard_map/all_gather | solution.py:254
  1128.7 7.5 convert_reduce_fusion
  1149.3 7.6 add_convert_fusion
  (209 shorter events, 142.9 us)
Async XLA Ops:
  2.7 5.3 copy-start.40
  2.7 5.3 copy-start.41
  10.3 4.2 copy-start.38
  10.3 7.5 copy-start.44
  10.3 73.6 %collective-permute-start = (bf16[1,2,512,768]{3,2,1,0:T(8,128)(2,1)}, bf16[1,2,512,768]{3,2,1,0:T(8,128)(2,1)}, u32[]{:S(2)}, u32[]{:S(2)}) collective-permute-start(bf16[1,2,512,768]{3,2,1,0:T(8,128)(2,1)} %bitcast.1), channel_id=1, source_target_pairs={{0,1},{1,0},{2,3},{3,2},{4,5},{5,4},{6,7},{7,6},{8,9},{9,8},{10,11... | collective-permute-start | bytes 4718600 | tf_op jit(solution)/shard_map/ppermute | solution.py:17
  14.5 69.3 %collective-permute-start.2 = (bf16[1,2,512,768]{3,2,1,0:T(8,128)(2,1)}, bf16[1,2,512,768]{3,2,1,0:T(8,128)(2,1)}, u32[]{:S(2)}, u32[]{:S(2)}) collective-permute-start(bf16[1,2,512,768]{3,2,1,0:T(8,128)(2,1)} %bitcast.19), channel_id=1, source_target_pairs={{0,1},{1,0},{2,3},{3,2},{4,5},{5,4},{6,7},{7,6},{8,9},{9,8},{10,11... | collective-permute-start | bytes 4718600 | tf_op jit(solution)/shard_map/ppermute | solution.py:17
  15.1 66.6 %collective-permute-start.1 = (bf16[1,2,512]{2,1,0:T(2,128)(2,1)}, bf16[1,2,512]{2,1,0:T(2,128)(2,1)}, u32[]{:S(2)}, u32[]{:S(2)}) collective-permute-start(bf16[1,2,512]{2,1,0:T(2,128)(2,1)} %convert_element_type.153), channel_id=1, source_target_pairs={{0,1},{1,0},{2,3},{3,2},{4,5},{5,4},{6,7},{7,6},{8,9},{9,8},{10,11... | collective-permute-start | bytes 6152 | tf_op jit(solution)/shard_map/ppermute | solution.py:17
  83.8 66.6 %copy-start.19 = (pred[2,12,512]{2,1,0:T(8,128)(4,1)}, pred[2,12,512]{2,1,0:T(8,128)(4,1)S(1)}, u32[]{:S(2)}) copy-start(pred[2,12,512]{2,1,0:T(8,128)(4,1)S(1)} %fusion.55) | copy-start | bytes 36868
  107.6 5.0 copy-start.15
  107.6 5.0 copy-start.16
  142.9 8.3 copy-start.1
  160.3 3.7 copy-start.45
  160.3 3.7 copy-start.46
  160.4 3.7 copy-start.49
  164.0 3.4 slice-start.3
  164.0 39.6 %slice-start = ((s8[4718592]{0:T(1024)(128)(4,1)}), s8[4194304]{0:T(1024)(128)(4,1)S(1)}, s32[]{:S(2)}) async-start(s8[4718592]{0:T(1024)(128)(4,1)} %bitcast.162), calls=%async_computation | async-start | bytes 8388608
  165.7 37.9 %copy-start.3 = (f32[1024,768]{1,0:T(8,128)}, f32[1024,768]{1,0:T(8,128)S(1)}, u32[]{:S(2)}) copy-start(f32[1024,768]{1,0:T(8,128)S(1)} %get-tuple-element.107) | copy-start | bytes 9437188
  165.8 80.1 %copy-start.21 = (f32[1024]{0:T(1024)}, f32[1024]{0:T(1024)S(1)}, u32[]{:S(2)}) copy-start(f32[1024]{0:T(1024)S(1)} %broadcast_multiply_fusion.1) | copy-start | bytes 12292
  168.4 77.5 %copy-start.23 = (f32[1024]{0:T(1024)}, f32[1024]{0:T(1024)S(1)}, u32[]{:S(2)}) copy-start(f32[1024]{0:T(1024)S(1)} %fusion.63) | copy-start | bytes 12292
  168.4 35.3 %slice-start.1 = ((s8[4718592]{0:T(1024)(128)(4,1)}), s8[524288]{0:T(1024)(128)(4,1)S(1)}, s32[]{:S(2)}) async-start(s8[4718592]{0:T(1024)(128)(4,1)} %bitcast.162), calls=%async_computation.1 | async-start | bytes 1048576
  168.4 35.3 %copy-start.50 = (f32[768]{0:T(1024)S(1)}, f32[768]{0:T(1024)}, u32[]{:S(2)}) copy-start(f32[768]{0:T(1024)} %param.33) | copy-start | bytes 9220
  203.6 5.5 copy-start.51
  234.2 11.7 %copy-start.4 = (f32[1024,768]{1,0:T(8,128)S(1)}, f32[1024,768]{1,0:T(8,128)}, u32[]{:S(2)}) copy-start(f32[1024,768]{1,0:T(8,128)} %copy-done.3) | copy-start | bytes 9437188
  245.9 3.1 copy-start.47
  251.7 6.6 copy-start.20
  258.2 23.0 %copy-start.18 = (f32[2,12,512]{2,1,0:T(8,128)S(1)}, f32[2,12,512]{2,1,0:T(8,128)}, u32[]{:S(2)}) copy-start(f32[2,12,512]{2,1,0:T(8,128)} %log_add_fusion) | copy-start | bytes 147460
  281.3 22.0 %copy-start.8 = (bf16[2,512,12,64]{1,0,3,2:T(2,128)(2,1)S(1)}, bf16[2,512,12,64]{1,0,3,2:T(2,128)(2,1)}, u32[]{:S(2)}) copy-start(bf16[2,512,12,64]{1,0,3,2:T(2,128)(2,1)} %fusion.42) | copy-start | bytes 4718596
  298.6 4.6 copy-start.2
  303.3 3.7 copy-start.7
  306.9 8.6 copy-start.14
  315.5 13.1 %copy-start.5 = (f32[1024,768]{1,0:T(8,128)S(1)}, f32[1024,768]{1,0:T(8,128)}, u32[]{:S(2)}) copy-start(f32[1024,768]{1,0:T(8,128)} %copy-done.3) | copy-start | bytes 9437188
  315.6 13.1 %copy-start.22 = (f32[1024]{0:T(1024)S(1)}, f32[1024]{0:T(1024)}, u32[]{:S(2)}) copy-start(f32[1024]{0:T(1024)} %copy-done.21) | copy-start | bytes 12292
  315.6 13.1 %copy-start.24 = (f32[1024]{0:T(1024)S(1)}, f32[1024]{0:T(1024)}, u32[]{:S(2)}) copy-start(f32[1024]{0:T(1024)} %copy-done.23) | copy-start | bytes 12292
  315.6 13.1 %copy-start.27 = (f32[768]{0:T(1024)S(1)}, f32[768]{0:T(1024)}, u32[]{:S(2)}) copy-start(f32[768]{0:T(1024)} %param.28) | copy-start | bytes 9220
  315.6 13.1 %copy-start.30 = (f32[768]{0:T(1024)S(1)}, f32[768]{0:T(1024)}, u32[]{:S(2)}) copy-start(f32[768]{0:T(1024)} %param.29) | copy-start | bytes 9220
  328.7 10.8 copy-start.10
  328.7 10.8 copy-start.37
  350.4 3.2 copy-start.25
  401.2 5.3 copy-start.13
  404.8 94.5 %collective-permute-start.3 = (bf16[1,2,512,768]{3,2,1,0:T(8,128)(2,1)}, bf16[1,2,512,768]{3,2,1,0:T(8,128)(2,1)}, u32[]{:S(2)}, u32[]{:S(2)}) collective-permute-start(bf16[1,2,512,768]{3,2,1,0:T(8,128)(2,1)} %fusion.39), channel_id=1, source_target_pairs={{0,1},{1,0},{2,3},{3,2},{4,5},{5,4},{6,7},{7,6},{8,9},{9,8},{10,11... | collective-permute-start | bytes 4718600 | tf_op jit(solution)/shard_map/ppermute | solution.py:17
  454.4 3.8 copy-start.6
  457.9 48.0 %collective-permute-start.4 = (bf16[1,2,512,768]{3,2,1,0:T(8,128)(2,1)}, bf16[1,2,512,768]{3,2,1,0:T(8,128)(2,1)}, u32[]{:S(2)}, u32[]{:S(2)}) collective-permute-start(bf16[1,2,512,768]{3,2,1,0:T(8,128)(2,1)} %fusion.40), channel_id=1, source_target_pairs={{0,1},{1,0},{2,3},{3,2},{4,5},{5,4},{6,7},{7,6},{8,9},{9,8},{10,11... | collective-permute-start | bytes 4718600 | tf_op jit(solution)/shard_map/ppermute | solution.py:17
  464.4 5.8 copy-start.43
  464.4 6.5 copy-start.42
  588.3 28.5 %copy-start.32 = (f32[16,48]{1,0:T(8,128)S(1)}, f32[16,48]{1,0:T(8,128)}, u32[]{:S(2)}) copy-start(f32[16,48]{1,0:T(8,128)} %reshape.525) | copy-start | bytes 9220
  588.3 29.9 %copy-start.31 = (f32[16,48]{1,0:T(8,128)S(1)}, f32[16,48]{1,0:T(8,128)}, u32[]{:S(2)}) copy-start(f32[16,48]{1,0:T(8,128)} %reshape.526) | copy-start | bytes 9220
  1136.2 13.1 %copy-start.36 = (f32[1024]{0:T(1024)S(1)}, f32[1024]{0:T(1024)}, u32[]{:S(2)}) copy-start(f32[1024]{0:T(1024)} %copy-done.34) | copy-start | bytes 12292
  1140.3 9.0 copy-start.12
  (13 other events, 26.3 us)
where the time goes:
time: 1170 us; the launch traced here: 1160 us
  blocking collectives  478 us (41%)
  local copies, waits for them, and re-layouts  332 us (28%)
  matrix products  216 us (18%)
  other arithmetic  78.8 us (7%)
  waiting for transfers between devices  49.9 us (4%)
    unnamed x1, blocking collectives  456 us
    unnamed x133, local copies, waits for them, and re-layouts  133 us
    ppermute x5, waiting for transfers between devices, from_partner(): return lax.ppermute(block, axis, route)  49.9 us
    dot_general x4, matrix products, contract_cols(): lax.dot_general(left_side, right_side, (((1,), (1,)), ((), ())), preferre...  39.4 us
    reshape x13, local copies, waits for them, and re-layouts, local(): gradient.reshape(batch_count, -1)  38.1 us
    dot_general x4, matrix products, contract_rows(): lax.dot_general(left_side, right_side, (((0,), (0,)), ((), ())), preferre...  36.4 us
    dot_general x1, matrix products, local(): jnp.dot(normed_low, w_in, preferred_element_type=jnp.float32) + bias_in  35.2 us
    reshape x1, local copies, waits for them, and re-layouts, local(): by_owner.reshape(batch_count * pair_count, span_width // pair_count)  28.2 us
  transfers between devices with their start and end apart: 5, of which 1 were waited for; matrix products, arithmetic and copies ran while one was open for 10% of the time, Pallas kernels for 0%

commit v1 on v0

v1 whole, which is shorter than its diff:
```python
import functools
import math

import jax
import jax.numpy as jnp
from jax import lax
from jax.experimental import pallas as pl
from jax.experimental.pallas import tpu as pltpu
from jax.sharding import PartitionSpec as P

EPSILON = 1e-05
BF = jnp.bfloat16
F32 = jnp.float32
VMEM_BYTES = 60 * 1024 * 1024
NEGATIVE = -1e30

SIDE, CORE, LIVE, OWNER, SOURCE = 0, 1, 2, 4, 5


def dot(a, b, ca=1, cb=0):
    return lax.dot_general(a, b, (((ca,), (cb,)), ((), ())), preferred_element_type=F32)


def params(**more):
    return pltpu.CompilerParams(vmem_limit_bytes=VMEM_BYTES, **more)


def cost(flops, read):
    return pl.CostEstimate(flops=int(flops), bytes_accessed=int(read), transcendentals=0)


def once(shape, index):
    return pl.BlockSpec(shape, index, pipeline_mode=pl.Buffered(1))


def mask_columns(mask_row):
    penalty = jnp.where(mask_row == 0, NEGATIVE, 0.0).astype(F32)
    return jnp.broadcast_to(penalty, (128, penalty.shape[1])).T


def project(with_queries, half_rows, meta, tok, mask, w_q, w_k, w_v, vec, *refs):
    q_t, k, k_t, v, v_t, mb = refs[-6:]
    rows = tok[...]
    keys = dot(rows, w_k[...]).astype(BF)
    k[...] = keys
    k_t[...] = keys.T
    values = (dot(rows, w_v[...]) + vec[1:2, :]).astype(BF)
    v[...] = values
    v_t[...] = values.T
    if with_queries:
        if half_rows:
            rows = tok[pl.ds(pl.multiple_of(meta[SIDE] * half_rows, half_rows), half_rows), :]
        queries = (dot(rows, w_q[...]) + vec[0:1, :]).astype(BF)
        q_t[...] = (queries * 0.125).T
    mb[...] = mask_columns(mask[...])


def pad_pair(part, half):
    zeros = jnp.zeros_like(part)
    return jnp.concatenate([part, zeros] if half == 0 else [zeros, part], axis=0)


def units(heads, size, total, meta):
    pair = pl.program_id(0)
    out = []
    for half in range(2):
        for slot, queries in enumerate((slice(0, size), slice(size, total))):
            source = meta[SOURCE + slot * heads + 2 * pair + half]
            out.append((half, slice(64 * half, 64 * half + 64), queries, source))
    return out


def attention_forward(heads, meta, q_t, k, v_t, mb, probs, att, att_t, inv):
    size, total = k.shape[1], q_t.shape[1]
    todo = units(heads, size, total, meta)

    def score(unit):
        half, span, queries, source = unit
        return dot(k[source], pad_pair(q_t[span, queries], half))

    def soften(unit, scores):
        half, span, queries, source = unit
        scores = scores + jnp.concatenate([mb[source]] * (scores.shape[1] // 128), axis=1)
        weights = jnp.exp(scores - jnp.max(scores, axis=0, keepdims=True))
        inverse = 1.0 / jnp.sum(weights, axis=0, keepdims=True)
        low = weights.astype(BF)
        probs[half, :, queries] = low
        inv[0, half : half + 1, queries] = inverse
        return low, inverse

    def attend(unit, soft):
        half, span, queries, source = unit
        att_t[span, queries] = (dot(v_t[source, span, :], soft[0]) * soft[1]).astype(BF)

    scores = {0: score(todo[0])}
    soft = {}
    for at in range(len(todo) + 1):
        if at + 1 < len(todo):
            scores[at + 1] = score(todo[at + 1])
        if at < len(todo):
            soft[at] = soften(todo[at], scores.pop(at))
        if at > 0:
            attend(todo[at - 1], soft.pop(at - 1))
    att[...] = att_t[...].T


def lane_sums(block):
    width = block.shape[1]
    part = block[:, :128]
    for at in range(128, width, 128):
        part = part + block[:, at : at + 128]
    return jnp.sum(part.T, axis=0, keepdims=True)


def attention_backward(
    heads, meta, probs, k_t, v, q_t, do_t, att_t, inv, gq_t, gk_t, gv_t, bq, bv, sum_k, sum_v, sum_q
):
    size, total = v.shape[1], q_t.shape[1]
    todo = units(heads, size, total, meta)
    sum_k[...] = jnp.zeros_like(sum_k)
    sum_v[...] = jnp.zeros_like(sum_v)

    def begin(unit):
        half, span, queries, source = unit
        scaled = do_t[span, queries].astype(F32) * inv[0, half : half + 1, queries]
        delta = jnp.sum(scaled * att_t[span, queries].astype(F32), axis=0, keepdims=True)
        scaled = scaled.astype(BF)
        return scaled, delta, dot(v[source], pad_pair(scaled, half))

    def middle(unit, begun):
        half, span, queries, source = unit
        scaled, delta, grad_probs = begun
        low = probs[half, :, queries]
        sum_v[source, span, :] += dot(scaled, low, 1, 1)
        return (low.astype(F32) * (grad_probs - delta)).astype(BF)

    def end(unit, grad_scores):
        half, span, queries, source = unit
        sum_k[source, span, :] += dot(q_t[span, queries], grad_scores, 1, 1)
        grad_q = dot(k_t[source, span, :], grad_scores) * 0.125
        sum_q[span, queries] = grad_q
        gq_t[span, queries] = grad_q.astype(BF)

    begun = {0: begin(todo[0])}
    grads = {}
    for at in range(len(todo) + 1):
        if at + 1 < len(todo):
            begun[at + 1] = begin(todo[at + 1])
        if at < len(todo):
            grads[at] = middle(todo[at], begun.pop(at))
        if at > 0:
            end(todo[at - 1], grads.pop(at - 1))
    gk_t[...] = sum_k[...].astype(BF)
    gv_t[...] = sum_v[...].astype(BF)
    bq[...] = lane_sums(sum_q[...])
    bv[...] = lane_sums(sum_v[0] + sum_v[1] + sum_v[2])


def normalise(rows):
    centred = rows - jnp.mean(rows, axis=-1, keepdims=True)
    scale = lax.rsqrt(jnp.mean(centred * centred, axis=-1, keepdims=True) + EPSILON)
    return centred * scale, scale


def norm_backward(grad, norm, scale, gain):
    scaled = grad * gain
    mean = jnp.mean(scaled, axis=-1, keepdims=True)
    along = jnp.mean(scaled * norm, axis=-1, keepdims=True)
    return scale * (scaled - mean - norm * along)


def gelu_pair(u):
    t = 1.0 / (1.0 + (0.3275911 * math.sqrt(0.5)) * jnp.abs(u))
    bell = jnp.exp(-0.5 * (u * u))
    poly = 0.5 * 1.061405429
    for factor in (-1.453152027, 1.421413741, -0.284496736, 0.254829592):
        poly = poly * t + 0.5 * factor
    tail = poly * t * bell
    below = jnp.where(u < 0, tail, 1.0 - tail)
    return u * below, below + u * (bell * (1.0 / math.sqrt(2.0 * math.pi)))


B_OUT, GAIN_ONE, SHIFT_ONE, B_BACK, GAIN_TWO, SHIFT_TWO = 2, 3, 4, 5, 6, 7


def tiles_of(total, tile):
    return [slice(at, at + tile) for at in range(0, total, tile)]


def split_cores(meta, block, keep, send, groups, rows):
    mine = meta[CORE]
    for at in range(groups):
        low = block[2 * at * rows : (2 * at + 1) * rows]
        high = block[(2 * at + 1) * rows : (2 * at + 2) * rows]
        keep[at] = jnp.where(mine == 0, low, high).astype(BF)
        send[at] = jnp.where(mine == 0, high, low).astype(BF)


def rows_forward(
    steps, meta, tok, tok_half, att, cot, cot_half, w_out, vec, w_in, b_in, w_back,
    slope, keep, send, sums, first_out, normed_out, mixed_out, second_out, back_out,
    first, normed_low, mixed, second, back_low, active, sems,
):
    step = pl.program_id(0)
    total = att.shape[0]
    tile = tok_half.shape[0]
    chunk = w_in.shape[1]
    tiles = tiles_of(total, tile)
    copies = [
        pltpu.make_async_copy(source, target, sems.at[at])
        for at, (source, target) in enumerate(
            ((first, first_out), (normed_low, normed_out), (mixed, mixed_out), (second, second_out), (back_low, back_out))
        )
    ]

    @pl.when(step == 0)
    def _():
        for at, span in enumerate(tiles):
            rows = (tok[span, :] if at + 1 < len(tiles) else tok_half[...]).astype(F32)
            rows = rows + dot(att[span, :], w_out[...]) + vec[B_OUT : B_OUT + 1, :]
            first[span, :] = rows
            result = normalise(rows)[0] * vec[GAIN_ONE : GAIN_ONE + 1, :] + vec[SHIFT_ONE : SHIFT_ONE + 1, :]
            normed_low[span, :] = result.astype(BF)
            second[span, :] = result + vec[B_BACK : B_BACK + 1, :]
        copies[0].start()
        copies[1].start()

    @pl.when(step < steps)
    def _():
        hidden = dot(normed_low[...], w_in[...]) + b_in[...]
        value, grad = gelu_pair(hidden)
        value = value.astype(BF)
        active[:, pl.ds(pl.multiple_of(step * chunk, chunk), chunk)] = value
        slope[...] = grad.astype(BF)
        second[...] += dot(value, w_back[...])

    @pl.when(step == steps - 1)
    def _():
        sums[...] = jnp.zeros_like(sums)
        gain, shift = vec[GAIN_TWO : GAIN_TWO + 1, :], vec[SHIFT_TWO : SHIFT_TWO + 1, :]
        for at, span in enumerate(tiles):
            last = at + 1 == len(tiles)
            live = meta[LIVE + last].astype(F32)
            norm, scale = normalise(second[span, :])
            mixed[span, :] = ((norm * gain + shift) * live).astype(BF)
            grad = (cot_half[...] if last else cot[span, :]).astype(F32) * live
            sums[0:1, :] += jnp.sum(grad * norm, axis=0, keepdims=True)
            sums[1:2, :] += jnp.sum(grad, axis=0, keepdims=True)
            grad = norm_backward(grad, norm, scale, gain)
            sums[2:3, :] += jnp.sum(grad, axis=0, keepdims=True)
            second[span, :] = grad
            back_low[span, :] = grad.astype(BF)
        for copy in copies[2:]:
            copy.start()

    @pl.when(step >= steps)
    def _():
        rows = keep.shape[1]
        columns = 2 * rows * keep.shape[0]
        part = active[:, pl.ds(pl.multiple_of((step - steps) * columns, columns), columns)]
        split_cores(meta, dot(part, back_low[...], 0, 0), keep, send, keep.shape[0], rows)

    @pl.when(step == pl.num_programs(0) - 1)
    def _():
        for copy in copies:
            copy.wait()


def rows_backward(
    meta, back_low, normed_low, slope, w_in, w_back, w_out, vec, first_in, second_in,
    keep, send, g_first, first_low, do_t, b_in, sums, first, g_normed, g_second, sems,
):
    step = pl.program_id(0)
    total = back_low.shape[0]
    tiles = tiles_of(total, total // 3)
    copies = [
        pltpu.make_async_copy(first_in, first, sems.at[0]),
        pltpu.make_async_copy(second_in, g_second, sems.at[1]),
    ]

    @pl.when(step == 0)
    def _():
        for copy in copies:
            copy.start()
        g_normed[...] = jnp.zeros_like(g_normed)

    grad = dot(back_low[...], w_back[...], 1, 1) * slope[...].astype(F32)
    b_in[...] = jnp.sum(grad, axis=0, keepdims=True)
    low = grad.astype(BF)
    g_normed[...] += dot(low, w_in[...], 1, 1)
    split_cores(meta, dot(normed_low[...], low, 0, 0), keep, send, keep.shape[0], keep.shape[1])

    @pl.when(step == pl.num_programs(0) - 1)
    def _():
        for copy in copies:
            copy.wait()
        sums[...] = jnp.zeros_like(sums)
        for span in tiles:
            norm, scale = normalise(first[span, :])
            grad = g_normed[span, :] + g_second[span, :]
            sums[0:1, :] += jnp.sum(grad * norm, axis=0, keepdims=True)
            sums[1:2, :] += jnp.sum(grad, axis=0, keepdims=True)
            grad = norm_backward(grad, norm, scale, vec[GAIN_ONE : GAIN_ONE + 1, :])
            sums[2:3, :] += jnp.sum(grad, axis=0, keepdims=True)
            g_first[span, :] = grad
            first_low[span, :] = grad.astype(BF)
        do_t[...] = dot(w_out[...], first_low[...], 1, 1).astype(BF)


def weight_gradients(per, meta, tok, tok_two, tok_two_half, tok_other, gq_t, gk_t, gv_t, att_t, first_low, rows, keep, send):
    step = pl.program_id(0)
    size = tok.shape[0]
    cut = keep.shape[2]

    def finish(block):
        split_cores(meta, block, keep, send, keep.shape[0], keep.shape[1])

    @pl.when(step < per)
    def _():
        finish(dot(tok[...], gq_t[:, :size], 0, 1) + dot(tok_two_half[...], gq_t[:, size:], 0, 1))

    for which, ref in ((1, gk_t), (2, gv_t)):

        @pl.when((step >= which * per) & (step < (which + 1) * per))
        def _():
            finish(
                dot(tok[...], ref[0], 0, 1) + dot(tok_two[...], ref[1], 0, 1) + dot(tok_other[...], ref[2], 0, 1)
            )

    @pl.when((step >= 3 * per) & (step < 4 * per))
    def _():
        finish(dot(att_t[...], first_low[...]))

    @pl.when(step == 4 * per)
    def _():
        vectors = rows[...]
        vectors = jnp.concatenate([vectors, jnp.zeros((cut - vectors.shape[0], vectors.shape[1]), F32)], axis=0)
        finish(vectors.T)


def tokens_sent(meta, w, gq_t, gk_t, gv_t, g_half, other, two, two_low):
    width = w.shape[0]
    half_rows = g_half.shape[0]
    total = dot(w[:, width : 2 * width], gk_t[1]) + dot(w[:, 2 * width :], gv_t[1])
    other[...] = total.T.astype(BF)
    total = dot(w[:, width : 2 * width], gk_t[0]) + dot(w[:, 2 * width :], gv_t[0])
    two[...] = total.T
    span = pl.ds(pl.multiple_of(meta[SIDE] * half_rows, half_rows), half_rows)
    two[span, :] += dot(w[:, :width], gq_t[...]).T + g_half[...]
    two_low[...] = two[...].astype(BF)


def tokens_kept(meta, w, gq_t, gk_t, gv_t, g_first, out):
    width = w.shape[0]
    total = dot(w[:, :width], gq_t[...]) + dot(w[:, width : 2 * width], gk_t[...]) + dot(w[:, 2 * width :], gv_t[...])
    out[...] = total.T + g_first[...]


def flip(value, axis, bit):
    count = lax.axis_size(axis)
    return lax.ppermute(value, axis, [(at, at ^ bit) for at in range(count)])


def after(value, *others):
    return lax.optimization_barrier((value,) + others)[0]


def add_halves(parts, meta, *refs):
    ins, outs = refs[: 4 * parts], refs[4 * parts :]
    for at in range(parts):
        kept, came, kept_other, came_other = ins[4 * at : 4 * at + 4]
        outs[2 * at][...] = (kept[...].astype(F32) + came[...].astype(F32)).astype(BF)
        outs[2 * at + 1][...] = (kept_other[...].astype(F32) + came_other[...].astype(F32)).astype(BF)


def combine(meta, arrays, splits):
    in_specs, operands, out_specs, shapes = [], [], [], []
    for (kept, came), (start, columns, bit, place) in zip(arrays, splits):
        count, rows, _ = kept.shape
        block = start // columns

        def index(flipped, i, m, bit=bit, place=place, block=block):
            mine = (m[OWNER] >> bit) & 1
            mine = 1 - mine if flipped else mine
            return ((((i >> place) << 1) | mine) << place) | (i & ((1 << place) - 1)), 0, block

        for flipped in (False, True):
            for array in (kept, came):
                in_specs.append(pl.BlockSpec((1, rows, columns), functools.partial(index, flipped)))
                operands.append(array)
        out_specs += [pl.BlockSpec((1, rows, columns), lambda i, m: (i, 0, 0))] * 2
        shapes += [jax.ShapeDtypeStruct((count // 2, rows, columns), BF)] * 2
    steps = arrays[0][0].shape[0] // 2
    out = pl.pallas_call(
        functools.partial(add_halves, len(splits)),
        grid_spec=pltpu.PrefetchScalarGridSpec(
            num_scalar_prefetch=1, grid=(steps,), in_specs=in_specs, out_specs=out_specs
        ),
        out_shape=shapes,
        compiler_params=params(),
        cost_estimate=cost(1e6, 3 * sum(2 * s.size for s in shapes)),
        name="combine",
    )(meta, *operands)
    return [(out[2 * at], out[2 * at + 1]) for at in range(len(splits))]


class Piece:
    def __init__(self, meta, keep, send, orders):
        self.meta, self.keep, self.orders = meta, keep, orders
        self.came = flip(send, "batch", 1)
        self.done = 0
        self.left = [sorted(order) for order in orders]

    def hop(self):
        if self.done == 0:
            columns = self.keep.shape[2] // len(self.orders)
            arrays = [(self.keep, self.came)] * len(self.orders)
            starts = [columns * at for at in range(len(self.orders))]
        else:
            arrays = list(zip(self.keep, self.came))
            columns = arrays[0][0].shape[2]
            starts = [0] * len(self.orders)
        if self.done < len(self.orders[0]):
            bits = [order[self.done] for order in self.orders]
            splits = [
                (start, columns, bit, left.index(bit)) for start, bit, left in zip(starts, bits, self.left)
            ]
            out = combine(self.meta, arrays, splits)
            self.keep = [kept for kept, _ in out]
            self.came = [flip(sent, "batch", 1 << bit) for (_, sent), bit in zip(out, bits)]
            for bit, left in zip(bits, self.left):
                left.remove(bit)
        elif self.done == len(self.orders[0]):
            self.keep = [
                (kept[0].astype(F32) + came[0].astype(F32)).astype(BF) for kept, came in arrays
            ]
            self.came = [flip(kept, "blk", 1) for kept in self.keep]
        self.done += 1
        return tuple(self.keep)

    def finish(self):
        while self.done <= len(self.orders[0]):
            self.hop()
        return [kept.astype(F32) + came.astype(F32) for kept, came in zip(self.keep, self.came)]


def local(
    tokens, cotangent, counts, perms, key_mask, w_qkv, bias_q, bias_v, w_out, bias_out, gain_one, shift_one,
    w_in, bias_in, w_back, bias_back, gain_two, shift_two,
):
    _, _, size, width = tokens.shape
    heads = perms.shape[1]
    pairs = heads // 2
    hidden = w_in.shape[1]
    half_rows = size // 2
    total = size + half_rows
    owners = lax.axis_size("batch")
    side = lax.axis_index("blk").astype(jnp.int32)
    owner = lax.axis_index("batch").astype(jnp.int32)
    whole = lambda *shape: once(shape, lambda *_: (0,) * len(shape))
    sds = jax.ShapeDtypeStruct
    anywhere = pl.BlockSpec(memory_space=pl.ANY)

    other_first = flip(tokens[0, 0], "blk", 1)
    other_mask = flip(key_mask[0], "blk", 1)
    came_two = lax.ppermute(tokens[0, 1], "blk", [(0, 1)])
    came_cot = lax.ppermute(cotangent[0, 1, half_rows:], "blk", [(0, 1)])

    count = counts[0]
    lookup = jnp.where(count == 2, perms[0], perms[1])
    own = jnp.where(side == 0, lookup[:, 0], lookup[:, 1])
    two = jnp.where(count > 2, lookup[:, 2], 2)
    source = jnp.concatenate([own, two])
    place = jnp.where(source == 2, 1, jnp.where(source == side, 0, 2))
    live = jnp.stack([(side < count).astype(jnp.int32), (count > 2).astype(jnp.int32)])
    meta = jnp.concatenate([jnp.stack([side, owner & 1]), live, owner[None], place])
    vec = jnp.stack([bias_q, bias_v, bias_out, gain_one, shift_one, bias_back, gain_two, shift_two])
    own_mask = key_mask[0]
    masks = jnp.stack([own_mask[0], jnp.where(side == 0, own_mask[1], other_mask[1]), other_mask[0]])[:, None]

    def grid_spec(grid, in_specs, out_specs, scratch=()):
        return pltpu.PrefetchScalarGridSpec(
            num_scalar_prefetch=1, grid=grid, in_specs=in_specs, out_specs=out_specs, scratch_shapes=list(scratch)
        )

    cut = 256
    per = width // cut
    kv_shapes = [
        sds((width, total), BF), sds((3, size, width), BF), sds((3, width, size), BF), sds((3, size, width), BF),
        sds((3, width, size), BF), sds((3, size, 128), F32),
    ]

    def run_projection(position, rows, mask, before):
        w_at = lambda base: pl.BlockSpec((width, cut), lambda g, m: (0, base * per + g))
        wide = pl.BlockSpec((None, size, cut), lambda g, m: (position, 0, g))
        tall = pl.BlockSpec((None, cut, size), lambda g, m: (position, g, 0))
        queries = (
            pl.BlockSpec((cut, half_rows), lambda g, m: (g, size // half_rows))
            if position == 1
            else pl.BlockSpec((cut, size), lambda g, m: (g, 0))
        )
        return pl.pallas_call(
            functools.partial(project, position != 2, half_rows if position == 1 else 0),
            grid_spec=grid_spec(
                (per,),
                [
                    whole(size, width),
                    pl.BlockSpec((None, 1, size), lambda g, m: (position, 0, 0)),
                    w_at(0), w_at(1), w_at(2),
                    pl.BlockSpec((8, cut), lambda g, m: (0, g)),
                ]
                + [anywhere] * len(before),
                [
                    anywhere if position == 2 else queries, wide, tall, wide, tall,
                    pl.BlockSpec((None, size, 128), lambda g, m: (position, 0, 0)),
                ],
            ),
            out_shape=kv_shapes,
            input_output_aliases={7 + n: n for n in range(len(before))},
            compiler_params=params(),
            cost_estimate=cost(2 * size * width * 2 * width, 10e6),
            name=f"project_{position}",
        )(meta, rows, mask, w_qkv, w_qkv, w_qkv, vec, *before)

    state = run_projection(0, tokens[0, 0], masks, [])
    state = run_projection(2, other_first, masks, state)
    tok_two = jnp.where(side == 0, tokens[0, 1], came_two)
    q_t, k, k_t, v, v_t, mb = run_projection(1, tok_two, masks, state)

    pair_q = pl.BlockSpec((128, total), lambda p, m: (p, 0))
    pair_rows = pl.BlockSpec((3, size, 128), lambda p, m: (0, 0, p))
    pair_cols = pl.BlockSpec((3, 128, size), lambda p, m: (0, p, 0))
    pair_probs = pl.BlockSpec((2, size, total), lambda p, m: (p, 0, 0))
    pair_inv = pl.BlockSpec((1, 2, total), lambda p, m: (p, 0, 0))
    probs, att, att_t, inv = pl.pallas_call(
        functools.partial(attention_forward, heads),
        grid_spec=grid_spec(
            (pairs,),
            [pair_q, pair_rows, pair_cols, whole(3, size, 128)],
            [pair_probs, pl.BlockSpec((total, 128), lambda p, m: (0, p)), pair_q, pair_inv],
        ),
        out_shape=[
            sds((heads, size, total), BF), sds((total, width), BF), sds((width, total), BF),
            sds((pairs, 2, total), F32),
        ],
        compiler_params=params(),
        cost_estimate=cost(8e9, 20e6),
        name="attention_forward",
    )(meta, q_t, k, v_t, mb)

    chunk = 512
    steps = hidden // chunk
    half = owners // 2
    back_rows = hidden // owners
    per_step = max(1, 192 // back_rows)
    flat = lambda dtype, columns=width: sds((total, columns), dtype)
    all_rows = whole(total, width)
    vectors = whole(8, width)
    side_rows = once((half_rows, width), lambda i, m: (m[SIDE], 0))
    early = lambda i: jnp.minimum(i, steps - 1)
    back_half = pl.BlockSpec((per_step, back_rows, width), lambda i, m: (jnp.maximum(i - steps, 0), 0, 0))
    cot_half = jnp.where(side == 0, cotangent[0, 1, :half_rows], came_cot)
    slope, back_keep, back_send, sums_two, first, normed_low, mixed, g_second, back_low = pl.pallas_call(
        functools.partial(rows_forward, steps),
        grid_spec=grid_spec(
            (steps + half // per_step,),
            [
                whole(size, width), side_rows, all_rows, whole(size, width), whole(half_rows, width),
                whole(width, width), vectors,
                pl.BlockSpec((width, chunk), lambda i, m: (0, early(i))),
                pl.BlockSpec((1, chunk), lambda i, m: (0, early(i))),
                pl.BlockSpec((chunk, width), lambda i, m: (early(i), 0)),
            ],
            [
                pl.BlockSpec((total, chunk), lambda i, m: (0, early(i))), back_half, back_half, whole(8, width),
            ] + [anywhere] * 5,
            [
                pltpu.VMEM((total, width), F32), pltpu.VMEM((total, width), BF), pltpu.VMEM((total, width), BF),
                pltpu.VMEM((total, width), F32), pltpu.VMEM((total, width), BF), pltpu.VMEM((total, hidden), BF),
                pltpu.SemaphoreType.DMA((5,)),
            ],
        ),
        out_shape=[
            flat(BF, hidden), sds((half, back_rows, width), BF), sds((half, back_rows, width), BF),
            sds((8, width), F32), flat(F32), flat(BF), flat(BF), flat(F32), flat(BF),
        ],
        compiler_params=params(),
        cost_estimate=cost(2 * total * width * (3 * hidden + width), 40e6),
        name="rows_forward",
    )(
        meta, tokens[0, 0], tok_two, att, cotangent[0, 0], cot_half, w_out, vec, w_in, bias_in.reshape(1, hidden),
        w_back,
    )

    bits = owners.bit_length() - 1
    turn = lambda first_bit: [1 + (first_bit + at) % (bits - 1) for at in range(bits - 1)]
    one_way = turn(0)
    other_way = [one_way[1], one_way[0]] + one_way[2:] if bits > 2 else one_way
    ways = [one_way, other_way]
    back = Piece(meta, back_keep, back_send, ways)
    mixed_came = lax.ppermute(mixed[size:], "blk", [(1, 0)])

    own_rows = width // owners
    in_half = lambda c: pl.BlockSpec((half, own_rows, c), lambda i, m: (0, 0, i))
    in_keep, in_send, g_first, first_low, do_t, g_b_in, sums_one = pl.pallas_call(
        rows_backward,
        grid_spec=grid_spec(
            (steps,),
            [
                all_rows, all_rows, pl.BlockSpec((total, chunk), lambda i, m: (0, i)),
                pl.BlockSpec((width, chunk), lambda i, m: (0, i)), pl.BlockSpec((chunk, width), lambda i, m: (i, 0)),
                whole(width, width), vectors, anywhere, anywhere,
            ],
            [
                in_half(chunk), in_half(chunk), all_rows, all_rows, whole(width, total),
                pl.BlockSpec((1, chunk), lambda i, m: (0, i)), whole(8, width),
            ],
            [
                pltpu.VMEM((total, width), F32), pltpu.VMEM((total, width), F32), pltpu.VMEM((total, width), F32),
                pltpu.SemaphoreType.DMA((2,)),
            ],
        ),
        out_shape=[
            sds((half, own_rows, hidden), BF), sds((half, own_rows, hidden), BF), flat(F32), flat(BF),
            sds((width, total), BF), sds((1, hidden), F32), sds((8, width), F32),
        ],
        compiler_params=params(),
        cost_estimate=cost(2 * total * width * (3 * hidden + width), 40e6),
        name="rows_backward",
    )(meta, back_low, normed_low, slope, w_in, w_back, w_out, vec, first, g_second)
    inner = Piece(meta, in_keep, in_send, ways)
    do_t = after(do_t, *back.hop())

    gq_t, gk_t, gv_t, g_bq, g_bv = pl.pallas_call(
        functools.partial(attention_backward, heads),
        grid_spec=grid_spec(
            (pairs,),
            [pair_probs, pair_cols, pair_rows, pair_q, pair_q, pair_q, pair_inv],
            [pair_q, pair_cols, pair_cols] + [pl.BlockSpec((1, 128), lambda p, m: (0, p))] * 2,
            [pltpu.VMEM((3, 128, size), F32), pltpu.VMEM((3, 128, size), F32), pltpu.VMEM((128, total), F32)],
        ),
        out_shape=[
            sds((width, total), BF), sds((3, width, size), BF), sds((3, width, size), BF), sds((1, width), F32),
            sds((1, width), F32),
        ],
        compiler_params=params(),
        cost_estimate=cost(14e9, 30e6),
        name="attention_backward",
    )(meta, probs, k_t, v, q_t, do_t, att_t, inv)
    gq_t = after(gq_t, *inner.hop())

    within = lambda base: (lambda i: jnp.clip(i - base * per, 0, per - 1))
    rows = jnp.concatenate(
        [sums_two[:3], sums_one[:3], g_bq, g_bv, g_b_in.reshape(width, -1).T, jnp.zeros((4, width), F32)], axis=0
    )
    at = lambda base: pl.BlockSpec((3, cut, size), lambda i, m: (0, within(base)(i), 0))
    qkv_keep, qkv_send = pl.pallas_call(
        functools.partial(weight_gradients, per),
        grid_spec=grid_spec(
            (4 * per + 1,),
            [
                whole(size, width), whole(size, width), side_rows, whole(size, width),
                pl.BlockSpec((cut, total), lambda i, m: (within(0)(i), 0)), at(1), at(2), whole(width, total),
                pl.BlockSpec((total, cut), lambda i, m: (0, within(3)(i))), whole(16, width),
            ],
            [in_half(cut), in_half(cut)],
        ),
        out_shape=[sds((half, own_rows, 4 * width + cut), BF)] * 2,
        compiler_params=params(),
        cost_estimate=cost(2 * size * width * width * 10, 25e6),
        name="weight_gradients",
    )(meta, tokens[0, 0], tok_two, tok_two, other_first, gq_t, gk_t, gv_t, att_t, first_low, rows)
    last = Piece(meta, qkv_keep, qkv_send, ways)
    gq_t = after(gq_t, qkv_keep, *back.hop())

    sent_shapes = [sds((size, width), BF), sds((size, width), F32), sds((size, width), BF)]
    last_two = lambda i, m: (0, 0, 0)
    sent_other, two_own, two_sent = pl.pallas_call(
        tokens_sent,
        grid_spec=grid_spec(
            (1,),
            [
                whole(width, 3 * width),
                pl.BlockSpec((width, half_rows), lambda i, m: (0, size // half_rows)),
                pl.BlockSpec((pl.Element(2), pl.Element(width), pl.Element(size)), lambda i, m: (1, 0, 0)),
                pl.BlockSpec((pl.Element(2), pl.Element(width), pl.Element(size)), lambda i, m: (1, 0, 0)),
                pl.BlockSpec((half_rows, width), lambda i, m: (size // half_rows, 0)),
            ],
            [whole(size, width)] * 3,
        ),
        out_shape=sent_shapes,
        compiler_params=params(),
        cost_estimate=cost(2 * size * width * width * 5, 12e6),
        name="tokens_sent",
    )(meta, w_qkv, gq_t, gk_t, gv_t, g_first)
    came_own = flip(sent_other, "blk", 1)
    came_two_grad = lax.ppermute(two_sent, "blk", [(1, 0)])
    own_grad = pl.pallas_call(
        tokens_kept,
        grid_spec=grid_spec(
            (1,),
            [
                whole(width, 3 * width), whole(width, size),
                pl.BlockSpec((None, width, size), lambda i, m: (0, 0, 0)),
                pl.BlockSpec((None, width, size), lambda i, m: (0, 0, 0)),
                whole(size, width),
            ],
            whole(size, width),
        ),
        out_shape=sds((size, width), F32),
        compiler_params=params(),
        cost_estimate=cost(2 * size * width * width * 3, 12e6),
        name="tokens_kept",
    )(meta, w_qkv, after(gq_t, *last.hop()), gk_t, gv_t, g_first)

    inner.hop()
    back.hop()
    last.hop()
    out_back = jnp.concatenate(back.finish(), axis=1)
    out_in = jnp.concatenate(inner.finish(), axis=1)
    out_last = jnp.concatenate(last.finish(), axis=1)

    tokens_grad = jnp.stack(
        [own_grad + came_own.astype(F32), jnp.where(side == 0, two_own + came_two_grad.astype(F32), 0.0)]
    ).astype(BF)[None]
    mixed_two = jnp.where(side == 0, jnp.concatenate([mixed[size:], mixed_came]), 0.0)
    mixed_all = jnp.stack([mixed[:size], mixed_two.astype(BF)])[None]
    pick = lambda at: out_last[:, 4 * width + at]
    return (
        mixed_all, tokens_grad,
        out_last[:, : 3 * width], pick(6), pick(7), out_last[:, 3 * width : 4 * width], pick(5), pick(3), pick(4),
        out_in, out_last[:, 4 * width + 8 : 4 * width + 8 + hidden // width].reshape(-1), out_back, pick(2), pick(0),
        pick(1),
    )


def solution(mesh):
    split = P("batch", None, "blk", None)
    in_specs = (split, split, P("batch"), P(), P("batch", None, "blk")) + (P(),) * 13
    matrix, vector = P("batch", None), P("batch")
    out_specs = (
        split, split, matrix, vector, vector, matrix, vector, vector, vector, matrix, vector, matrix, vector, vector,
        vector,
    )
    return jax.shard_map(local, mesh=mesh, in_specs=in_specs, out_specs=out_specs, check_vma=False)
```

time: 1170 us -> 341 us (0.29)
  blocking collectives: 478 us -> 0 us
  local copies, waits for them, and re-layouts: 332 us -> 26.5 us
  matrix products: 216 us -> 0 us
  Pallas kernels: 0 us -> 165 us
  other arithmetic: 78.8 us -> 14.3 us
  waiting for transfers between devices: 49.9 us -> 89.7 us
  starting transfers between devices: 6.99 us -> 41 us
    unnamed x1 -> x0, blocking collectives: 456 us -> none
    dot_general x23 -> x0, matrix products: 216 us -> none  [the longest x4 39.4 us: contract_cols(): lax.dot_general(left_side, right_side, (((1,), (1,)), ((), ())), preferre...]
    pallas_call x0 -> x19, Pallas kernels: none -> 165 us  [the longest x9 34.5 us: combine(): pl.pallas_call(functools.partial(add_halves, len(splits)), grid_spec=pltp...]
    unnamed x133 -> x77, local copies, waits for them, and re-layouts: 133 us -> 10.4 us
    reshape x23 -> x3, local copies, waits for them, and re-layouts: 101 us -> 1.21 us  [the longest x1 0.67 us: local(): out_last[:, 4 * width + 8:4 * width + 8 + hidden // width].reshape(-1)]
    ppermute x5 -> x34, waiting for transfers between devices: 49.9 us -> 89.7 us  [the longest x30 58 us: flip(): return lax.ppermute(value, axis, [(at, at ^ bit) for at in range(count)])]
    another operation x7 -> x10, local copies, waits for them, and re-layouts: 35.9 us -> 1.87 us  [the longest x1 1.18 us: local(): mixed_all = jnp.stack([mixed[:size], mixed_two.astype(BF)])[None]]
    ppermute x5 -> x34, starting transfers between devices: 6.99 us -> 41 us  [the longest x30 31.6 us: flip(): return lax.ppermute(value, axis, [(at, at ^ bit) for at in range(count)])]
  transfers between devices with their start and end apart: 5 -> 34, of which waited for: 1 -> 12; matrix products, arithmetic and copies ran while one was open for 10% -> 9% of each run, Pallas kernels for 0% -> 32%
where the time goes in v1:
time: 341 us; the launch traced here: 339 us
  Pallas kernels  165 us (48%)
  waiting for transfers between devices  89.7 us (26%)
  starting transfers between devices  41 us (12%)
  local copies, waits for them, and re-layouts  26.5 us (8%)
  other arithmetic  14.3 us (4%)
    ppermute x30, waiting for transfers between devices, flip(): return lax.ppermute(value, axis, [(at, at ^ bit) for at in range(count)])  58 us
    pallas_call x9, Pallas kernels, combine(): pl.pallas_call(functools.partial(add_halves, len(splits)), grid_spec=pltp...  34.5 us
    ppermute x30, starting transfers between devices, flip(): return lax.ppermute(value, axis, [(at, at ^ bit) for at in range(count)])  31.6 us
    pallas_call x1, Pallas kernels, local(): pl.pallas_call(functools.partial(rows_forward, steps), grid_spec=grid_spe...  30.4 us
    ppermute x1, waiting for transfers between devices, local(): came_cot = lax.ppermute(cotangent[0, 1, half_rows:], 'blk', [(0, 1)])  24.6 us
    pallas_call x1, Pallas kernels, local(): pl.pallas_call(rows_backward, grid_spec=grid_spec((steps,), [all_rows, al...  22.4 us
    pallas_call x3, Pallas kernels, run_projection(): pl.pallas_call(functools.partial(project, position != 2, half_rows if pos...  19.6 us
    pallas_call x1, Pallas kernels, local(): pl.pallas_call(functools.partial(weight_gradients, per), grid_spec=grid_s...  15.6 us
  transfers between devices with their start and end apart: 34, of which 12 were waited for; matrix products, arithmetic and copies ran while one was open for 9% of the time, Pallas kernels for 32%

profile of v1, /device:TPU:0, one launch (start us, length us, event | category | flops | bytes accessed | tf_op | source)
XLA Modules:
  0.0 338.8 jit_solution(4630655364387411767)
XLA Ops:
  0.7 3.0 collective-permute-start.1
  3.7 2.4 slice_bitcast_fusion.2
  6.3 4.7 %collective-permute-start = (bf16[512,768]{1,0:T(8,128)(2,1)}, bf16[512,768]{1,0:T(8,128)(2,1)}, u32[]{:S(2)}, u32[]{:S(2)}) collective-permute-start(bf16[512,768]{1,0:T(8,128)(2,1)} %get-tuple-element.199), channel_id=1, source_target_pairs={{0,1},{2,3},{4,5},{6,7},{8,9},{10,11},{12,13},{14,15},{16,17},{18,... | collective-permute-start | bytes 2359304 | tf_op jit(solution)/shard_map/ppermute | solution.py:466
  11.0 2.0 collective-permute-start.3
  16.9 6.8 %project_0.1 = (bf16[768,768]{1,0:T(8,128)(2,1)}, bf16[3,512,768]{2,1,0:T(8,128)(2,1)}, bf16[3,768,512]{2,1,0:T(8,128)(2,1)}, bf16[3,512,768]{2,1,0:T(8,128)(2,1...) custom-call(s32[29]{0:T(128)} %concatenate.41.meta, bf16[512,768]{1,0:T(8,128)(2,1)} %copy-done.4, ...), custom_call_target="tpu_custom_call" | custom-call | flops 1207959552 | bytes 10000000 | tf_op jit(solution)/shard_map/project_0/pallas_call | solution.py:502
  23.7 24.6 %collective-permute-done.3 = bf16[256,768]{1,0:T(8,128)(2,1)} collective-permute-done((bf16[256,768]{1,0:T(8,128)(2,1)S(1)}, bf16[256,768]{1,0:T(8,128)(2,1)}, u32[]{:S(2)}, u32[]{:S(2)}) %collective-permute-start.3) | collective-permute-done | bytes 393248 | tf_op jit(solution)/shard_map/ppermute | solution.py:467
  48.4 1.8 bitcast_select_fusion.cot_half
  52.1 6.4 %project_2.1 = (bf16[768,768]{1,0:T(8,128)(2,1)}, bf16[3,512,768]{2,1,0:T(8,128)(2,1)}, bf16[3,768,512]{2,1,0:T(8,128)(2,1)}, bf16[3,512,768]{2,1,0:T(8,128)(2,1...) custom-call(s32[29]{0:T(128)} %concatenate.41.meta, ...), custom_call_target="tpu_custom_call", output_to_operand_aliasing={{0}: (7, {}), {1}: (8, {}), {2}: (9, {}), {3}: (10, {}), {4... | custom-call | flops 1207959552 | bytes 10000000 | tf_op jit(solution)/shard_map/project_2/pallas_call | solution.py:502
  58.4 6.4 %project_1.1 = (bf16[768,768]{1,0:T(8,128)(2,1)}, bf16[3,512,768]{2,1,0:T(8,128)(2,1)}, bf16[3,768,512]{2,1,0:T(8,128)(2,1)}, bf16[3,512,768]{2,1,0:T(8,128)(2,1...) custom-call(s32[29]{0:T(128)} %concatenate.41.meta, ...), custom_call_target="tpu_custom_call", output_to_operand_aliasing={{0}: (7, {}), {1}: (8, {}), {2}: (9, {}), {3}: (10, {}), {4... | custom-call | flops 1207959552 | bytes 10000000 | tf_op jit(solution)/shard_map/project_1/pallas_call | solution.py:502
  64.9 12.1 %attention_forward.1 = (bf16[12,512,768]{2,1,0:T(8,128)(2,1)}, bf16[768,768]{1,0:T(8,128)(2,1)}, bf16[768,768]{1,0:T(8,128)(2,1)}, f32[6,2,768]{2,1,0:T(2,128)}) custom-call(s32[29]{0:T(128)} %concatenate.41.meta, bf16[768,768]{1,0:T(8,128)(2,1)} %get-tuple-element.115.q_t, bf16[3,512,768]{2,1,0:T(8,128)(2,1)} %get-tuple-element.116.k, ...), custom_call_target="tpu_custom_call" | custom-call | flops 8000000000 | bytes 20000000 | tf_op jit(solution)/shard_map/attention_forward/pallas_call | solution.py:535
  76.9 30.4 %rows_forward.1 = (bf16[768,3072]{1,0:T(8,128)(2,1)}, bf16[8,192,768]{2,1,0:T(8,128)(2,1)}, bf16[8,192,768]{2,1,0:T(8,128)(2,1)}, f32[8,768]{1,0:T(8,128)}, f32[...) custom-call(s32[29]{0:T(128)} %concatenate.41.meta, ...), custom_call_target="tpu_custom_call" | custom-call | flops 11777605632 | bytes 40000000 | tf_op jit(solution)/shard_map/rows_forward/pallas_call | solution.py:563
  107.4 22.4 %rows_backward.1 = (bf16[8,48,3072]{2,1,0:T(8,128)(2,1)}, bf16[8,48,3072]{2,1,0:T(8,128)(2,1)}, f32[768,768]{1,0:T(8,128)}, bf16[768,768]{1,0:T(8,128)(2,1)}, bf...) custom-call(s32[29]{0:T(128)} %concatenate.41.meta, bf16[768,768]{1,0:T(8,128)(2,1)} %get-tuple-element.124.back_low, ...), custom_call_target="tpu_custom_call" | custom-call | flops 11777605632 | bytes 40000000 | tf_op jit(solution)/shard_map/rows_backward/pallas_call | solution.py:605
  130.4 1.8 slice_bitcast_fusion.6
  139.8 7.0 %collective-permute-done.4 = bf16[256,768]{1,0:T(8,128)(2,1)S(1)} collective-permute-done((bf16[256,768]{1,0:T(8,128)(2,1)}, bf16[256,768]{1,0:T(8,128)(2,1)S(1)}, u32[]{:S(2)}, u32[]{:S(2)}) %collective-permute-start.4) | collective-permute-done | bytes 393248 | tf_op jit(solution)/shard_map/ppermute | solution.py:601
  148.3 5.2 %combine.9 = (bf16[4,192,384]{2,1,0:T(8,128)(2,1)}, bf16[4,192,384]{2,1,0:T(8,128)(2,1)}, bf16[4,192,384]{2,1,0:T(8,128)(2,1)}, bf16[4,192,384]{2,1,0:T(8,128)(2,1)}) custom-call(s32[29]{0:T(128)} %concatenate.41.meta, bf16[8,192,768]{2,1,0:T(8,128)(2,1)} %get-tuple-element.130.refs_0_.refs_2_.refs_4_.refs_6_, ...), custom_call_target="tpu_custom_call" | custom-call | flops 1000000 | bytes 7077888 | tf_op jit(solution)/shard_map/combine/pallas_call | solution.py:394
  153.4 1.9 collective-permute-start.7
  155.3 1.6 collective-permute-start.8
  158.3 5.1 %combine.10 = (bf16[4,48,1536]{2,1,0:T(8,128)(2,1)}, bf16[4,48,1536]{2,1,0:T(8,128)(2,1)}, bf16[4,48,1536]{2,1,0:T(8,128)(2,1)}, bf16[4,48,1536]{2,1,0:T(8,128)(2,1)}) custom-call(s32[29]{0:T(128)} %concatenate.41.meta, bf16[8,48,3072]{2,1,0:T(8,128)(2,1)} %get-tuple-element.138.refs_0_.refs_2_.refs_4_.refs_6_, bf16[8,48,3072]{2,1,0:T(8,128)(2,1)} %copy-done.1, ...), custom_call_target="tpu_custom_call" | custom-call | flops 1000000 | bytes 7077888 | tf_op jit(solution)/shard_map/combine/pallas_call | solution.py:394
  164.1 14.8 %attention_backward.1 = (bf16[768,768]{1,0:T(8,128)(2,1)}, bf16[3,768,512]{2,1,0:T(8,128)(2,1)}, bf16[3,768,512]{2,1,0:T(8,128)(2,1)}, f32[1,768]{1,0:T(1,128)}, f32[1,768]{1,0:T(1,128)}) custom-call(s32[29]{0:T(128)} %concatenate.41.meta, bf16[12,512,768]{2,1,0:T(8,128)(2,1)} %get-tuple-element.121.probs, bf16[3,768,512]{2,1,0:T(8,128)(2,1)} %get-tuple-element.122.k_t, ...), custom_call_target="tpu_custom_call" | custom-call | flops 14000000000 | bytes 30000000 | tf_op jit(solution)/shard_map/attention_backward/pallas_call | solution.py:634
  179.0 1.9 concatenate.45.rows
  182.6 3.3 combine.11
  185.9 1.9 collective-permute-start.28
  187.8 1.5 collective-permute-start.29
  191.0 3.3 combine.15
  195.0 15.6 %weight_gradients.1 = (bf16[8,48,3328]{2,1,0:T(8,128)(2,1)}, bf16[8,48,3328]{2,1,0:T(8,128)(2,1)}) custom-call(s32[29]{0:T(128)} %concatenate.41.meta, bf16[512,768]{1,0:T(8,128)(2,1)} %copy-done.4, bf16[512,768]{1,0:T(8,128)(2,1)} %broadcast_select_fusion.tok.tok_half.tok_two.tok_two_half, ...), custom_call_target="tpu_custom_call" | custom-call | flops 6039797760 | bytes 25000000 | tf_op jit(solution)/shard_map/weight_gradients/pallas_call | solution.py:657
  211.4 2.9 combine.16
  214.2 2.9 collective-permute-start.24
  217.1 8.6 %tokens_sent.1 = (bf16[512,768]{1,0:T(8,128)(2,1)}, f32[512,768]{1,0:T(8,128)}, bf16[512,768]{1,0:T(8,128)(2,1)}) custom-call(s32[29]{0:T(128)} %concatenate.41.meta, bf16[768,2304]{1,0:T(8,128)(2,1)} %w.3, bf16[768,768]{1,0:T(8,128)(2,1)} %get-tuple-element.160.gq_t, bf16[3,768,512]{2,1,0:T(8,128)(2,1)} %get-tuple-element.143.gk_t, ...), custom_call_target="tpu_custom_call" | custom-call | flops 3019898880 | bytes 12000000 | tf_op jit(solution)/shard_map/tokens_sent/pallas_call | solution.py:678
  225.8 1.4 collective-permute-start.11
  227.9 2.8 combine.17
  230.8 2.9 collective-permute-start.32
  233.7 11.1 %collective-permute-done.30 = bf16[1,192,384]{2,1,0:T(8,128)(2,1)S(1)} collective-permute-done((bf16[1,192,384]{2,1,0:T(8,128)(2,1)}, bf16[1,192,384]{2,1,0:T(8,128)(2,1)S(1)}, u32[]{:S(2)}, u32[]{:S(2)}) %collective-permute-start.30) | collective-permute-done | bytes 147488 | tf_op jit(solution)/shard_map/ppermute | solution.py:361
  245.8 7.8 %collective-permute-done.26 = bf16[1,48,1536]{2,1,0:T(8,128)(2,1)S(1)} collective-permute-done((bf16[1,48,1536]{2,1,0:T(8,128)(2,1)S(1)}, bf16[1,48,1536]{2,1,0:T(8,128)(2,1)S(1)}, u32[]{:S(2)}, u32[]{:S(2)}) %collective-permute-start.26) | collective-permute-done | bytes 147488 | tf_op jit(solution)/shard_map/ppermute | solution.py:361
  253.6 3.3 collective-permute-start.31
  258.0 10.7 %collective-permute-done.25 = bf16[48,1536]{1,0:T(8,128)(2,1)S(1)} collective-permute-done((bf16[48,1536]{1,0:T(8,128)(2,1)S(1)}, bf16[48,1536]{1,0:T(8,128)(2,1)S(1)}, u32[]{:S(2)}, u32[]{:S(2)}) %collective-permute-start.25) | collective-permute-done | bytes 147488 | tf_op jit(solution)/shard_map/ppermute | solution.py:361
  268.8 5.1 %collective-permute-done.27 = bf16[48,1536]{1,0:T(8,128)(2,1)S(1)} collective-permute-done((bf16[48,1536]{1,0:T(8,128)(2,1)S(1)}, bf16[48,1536]{1,0:T(8,128)(2,1)S(1)}, u32[]{:S(2)}, u32[]{:S(2)}) %collective-permute-start.27) | collective-permute-done | bytes 147488 | tf_op jit(solution)/shard_map/ppermute | solution.py:361
  274.3 1.5 copy-done
  275.8 5.5 %combine.12 = (bf16[4,48,1664]{2,1,0:T(8,128)(2,1)}, bf16[4,48,1664]{2,1,0:T(8,128)(2,1)}, bf16[4,48,1664]{2,1,0:T(8,128)(2,1)}, bf16[4,48,1664]{2,1,0:T(8,128)(2,1)}) custom-call(s32[29]{0:T(128)} %concatenate.41.meta, bf16[8,48,3328]{2,1,0:T(8,128)(2,1)} %get-tuple-element.151.refs_0_.refs_2_.refs_4_.refs_6_, bf16[8,48,3328]{2,1,0:T(8,128)(2,1)} %copy-done, ...), custom_call_target="tpu_custom_call" | custom-call | flops 1000000 | bytes 7667712 | tf_op jit(solution)/shard_map/combine/pallas_call | solution.py:394
  281.2 1.6 collective-permute-start.12
  282.8 1.6 collective-permute-start.13
  286.1 10.2 %collective-permute-done.12.refs_1_.refs_3_ = bf16[4,48,1664]{2,1,0:T(8,128)(2,1)S(1)} collective-permute-done((bf16[4,48,1664]{2,1,0:T(8,128)(2,1)}, bf16[4,48,1664]{2,1,0:T(8,128)(2,1)S(1)}, u32[]{:S(2)}, u32[]{:S(2)}) %collective-permute-start.12) | collective-permute-done | bytes 639008 | tf_op jit(solution)/shard_map/ppermute | solution.py:361
  298.4 3.5 %combine.13 = (bf16[2,48,1664]{2,1,0:T(8,128)(2,1)}, bf16[2,48,1664]{2,1,0:T(8,128)(2,1)}, bf16[2,48,1664]{2,1,0:T(8,128)(2,1)}, bf16[2,48,1664]{2,1,0:T(8,128)(2,1)}) custom-call(s32[29]{0:T(128)} %concatenate.41.meta, bf16[4,48,1664]{2,1,0:T(8,128)(2,1)} %get-tuple-element.158.refs_0_.refs_2_, bf16[4,48,1664]{2,1,0:T(8,128)(2,1)} %copy-done.5, ...), custom_call_target="tpu_custom_call" | custom-call | flops 1000000 | bytes 3833856 | tf_op jit(solution)/shard_map/combine/pallas_call | solution.py:394
  301.9 1.6 collective-permute-start.14
  305.4 7.3 %tokens_kept.1 = f32[512,768]{1,0:T(8,128)} custom-call(s32[29]{0:T(128)} %concatenate.41.meta, bf16[768,2304]{1,0:T(8,128)(2,1)} %w.3, bf16[768,768]{1,0:T(8,128)(2,1)} %get-tuple-element.160.gq_t, bf16[3,768,512]{2,1,0:T(8,128)(2,1)} %get-tuple-element.143.gk_t, bf16[3,768,512]{2,1,0:T(8,128)(2,1)} %get-tuple-element.144.gv_t, ...), custom_call_target="tpu_custom_call" | custom-call | flops 1811939328 | bytes 12000000 | tf_op jit(solution)/shard_map/tokens_kept/pallas_call | solution.py:698
  313.5 3.0 combine.14
  319.4 2.6 collective-permute-start.16
  322.0 6.7 %collective-permute-done.18 = bf16[1,48,1664]{2,1,0:T(8,128)(2,1)S(1)} collective-permute-done((bf16[1,48,1664]{2,1,0:T(8,128)(2,1)}, bf16[1,48,1664]{2,1,0:T(8,128)(2,1)S(1)}, u32[]{:S(2)}, u32[]{:S(2)}) %collective-permute-start.18) | collective-permute-done | bytes 159776 | tf_op jit(solution)/shard_map/ppermute | solution.py:361
  331.5 4.0 %collective-permute-done.19 = bf16[48,1664]{1,0:T(8,128)(2,1)S(1)} collective-permute-done((bf16[48,1664]{1,0:T(8,128)(2,1)S(1)}, bf16[48,1664]{1,0:T(8,128)(2,1)S(1)}, u32[]{:S(2)}, u32[]{:S(2)}) %collective-permute-start.19) | collective-permute-done | bytes 159776 | tf_op jit(solution)/shard_map/ppermute | solution.py:361
  (172 shorter events, 40.4 us)
Async XLA Ops:
  0.6 10.3 %copy-start.11 = (bf16[1,2,512,768]{3,2,1,0:T(8,128)(2,1)S(1)}, bf16[1,2,512,768]{3,2,1,0:T(8,128)(2,1)}, u32[]{:S(2)}) copy-start(bf16[1,2,512,768]{3,2,1,0:T(8,128)(2,1)} %param.19) | copy-start | bytes 4718596
  0.7 12.4 %copy-start.34 = (s32[1,2,512]{2,1,0:T(2,128)S(1)}, s32[1,2,512]{2,1,0:T(2,128)}, u32[]{:S(2)}) copy-start(s32[1,2,512]{2,1,0:T(2,128)} %param.22) | copy-start | bytes 12292
  0.7 15.6 %collective-permute-start.1 = (s32[2,512]{1,0:T(2,128)}, s32[2,512]{1,0:T(2,128)S(1)}, u32[]{:S(2)}, u32[]{:S(2)}) collective-permute-start(s32[2,512]{1,0:T(2,128)} %bitcast.61), channel_id=1, source_target_pairs={{0,1},{1,0},{2,3},{3,2},{4,5},{5,4},{6,7},{7,6},{8,9},{9,8},{10,11... | collective-permute-start | bytes 12296 | tf_op jit(solution)/shard_map/ppermute | solution.py:361
  6.0 10.9 %copy-start.4 = (bf16[512,768]{1,0:T(8,128)(2,1)}, bf16[512,768]{1,0:T(8,128)(2,1)S(1)}, u32[]{:S(2)}) copy-start(bf16[512,768]{1,0:T(8,128)(2,1)S(1)} %get-tuple-element.200.tok) | copy-start | bytes 2359300
  6.1 8.8 %copy-start.30 = (f32[768]{0:T(1024)S(1)}, f32[768]{0:T(1024)}, u32[]{:S(2)}) copy-start(f32[768]{0:T(1024)} %param.29) | copy-start | bytes 9220
  6.1 8.9 %copy-start.31 = (f32[768]{0:T(1024)S(1)}, f32[768]{0:T(1024)}, u32[]{:S(2)}) copy-start(f32[768]{0:T(1024)} %param.33) | copy-start | bytes 9220
  6.1 8.9 %copy-start.32 = (f32[768]{0:T(1024)S(1)}, f32[768]{0:T(1024)}, u32[]{:S(2)}) copy-start(f32[768]{0:T(1024)} %param.34) | copy-start | bytes 9220
  6.1 8.9 %copy-start.33 = (f32[768]{0:T(1024)S(1)}, f32[768]{0:T(1024)}, u32[]{:S(2)}) copy-start(f32[768]{0:T(1024)} %param.35) | copy-start | bytes 9220
  6.1 45.0 %collective-permute-start.2 = (bf16[512,768]{1,0:T(8,128)(2,1)S(1)}, bf16[512,768]{1,0:T(8,128)(2,1)S(1)}, u32[]{:S(2)}, u32[]{:S(2)}) collective-permute-start(bf16[512,768]{1,0:T(8,128)(2,1)S(1)} %get-tuple-element.200.tok), channel_id=1, source_target_pairs={{0,1},{1,0},{2,3},{3,2},{4,5},{5,4},{6,7},{7,6},{8,9},{9,8},{10,11... | collective-permute-start | bytes 2359304 | tf_op jit(solution)/shard_map/ppermute | solution.py:361
  6.3 43.9 %collective-permute-start = (bf16[512,768]{1,0:T(8,128)(2,1)}, bf16[512,768]{1,0:T(8,128)(2,1)}, u32[]{:S(2)}, u32[]{:S(2)}) collective-permute-start(bf16[512,768]{1,0:T(8,128)(2,1)} %get-tuple-element.199), channel_id=1, source_target_pairs={{0,1},{2,3},{4,5},{6,7},{8,9},{10,11},{12,13},{14,15},{16,17},{18,... | collective-permute-start | bytes 2359304 | tf_op jit(solution)/shard_map/ppermute | solution.py:466
  11.0 37.4 %collective-permute-start.3 = (bf16[256,768]{1,0:T(8,128)(2,1)S(1)}, bf16[256,768]{1,0:T(8,128)(2,1)}, u32[]{:S(2)}, u32[]{:S(2)}) collective-permute-start(bf16[256,768]{1,0:T(8,128)(2,1)S(1)} %slice_bitcast_fusion.4), channel_id=1, source_target_pairs={{0,1},{2,3},{4,5},{6,7},{8,9},{10,11},{12,13},{14,15},{16,17},{18,... | collective-permute-start | bytes 1179656 | tf_op jit(solution)/shard_map/ppermute | solution.py:467
  16.9 33.3 %copy-start.3 = (bf16[1,2,512,768]{3,2,1,0:T(8,128)(2,1)S(1)}, bf16[1,2,512,768]{3,2,1,0:T(8,128)(2,1)}, u32[]{:S(2)}) copy-start(bf16[1,2,512,768]{3,2,1,0:T(8,128)(2,1)} %param.18) | copy-start | bytes 4718596
  107.4 40.9 %collective-permute-start.5 = (bf16[8,192,768]{2,1,0:T(8,128)(2,1)}, bf16[8,192,768]{2,1,0:T(8,128)(2,1)}, u32[]{:S(2)}, u32[]{:S(2)}) collective-permute-start(bf16[8,192,768]{2,1,0:T(8,128)(2,1)} %get-tuple-element.131), channel_id=1, source_target_pairs={{0,2},{2,0},{4,6},{6,4},{8,10},{10,8},{12,14},{14,12},{16,18},{18,... | collective-permute-start | bytes 7077896 | tf_op jit(solution)/shard_map/ppermute | solution.py:361
  129.9 27.0 %collective-permute-start.6 = (bf16[8,48,3072]{2,1,0:T(8,128)(2,1)}, bf16[8,48,3072]{2,1,0:T(8,128)(2,1)S(1)}, u32[]{:S(2)}, u32[]{:S(2)}) collective-permute-start(bf16[8,48,3072]{2,1,0:T(8,128)(2,1)} %get-tuple-element.139), channel_id=1, source_target_pairs={{0,2},{2,0},{4,6},{6,4},{8,10},{10,8},{12,14},{14,12},{16,18},{18,... | collective-permute-start | bytes 7077896 | tf_op jit(solution)/shard_map/ppermute | solution.py:361
  132.2 14.6 %collective-permute-start.4 = (bf16[256,768]{1,0:T(8,128)(2,1)}, bf16[256,768]{1,0:T(8,128)(2,1)S(1)}, u32[]{:S(2)}, u32[]{:S(2)}) collective-permute-start(bf16[256,768]{1,0:T(8,128)(2,1)} %get-tuple-element.202), channel_id=1, source_target_pairs={{1,0},{3,2},{5,4},{7,6},{9,8},{11,10},{13,12},{15,14},{17,16},{19,... | collective-permute-start | bytes 1179656 | tf_op jit(solution)/shard_map/ppermute | solution.py:601
  153.4 27.5 %collective-permute-start.7 = (bf16[4,192,384]{2,1,0:T(8,128)(2,1)}, bf16[4,192,384]{2,1,0:T(8,128)(2,1)S(1)}, u32[]{:S(2)}, u32[]{:S(2)}) collective-permute-start(bf16[4,192,384]{2,1,0:T(8,128)(2,1)} %get-tuple-element.152), channel_id=1, source_target_pairs={{0,4},{2,6},{4,0},{6,2},{8,12},{10,14},{12,8},{14,10},{16,20},{18,... | collective-permute-start | bytes 1769480 | tf_op jit(solution)/shard_map/ppermute | solution.py:361
  155.3 25.7 %collective-permute-start.8 = (bf16[4,192,384]{2,1,0:T(8,128)(2,1)}, bf16[4,192,384]{2,1,0:T(8,128)(2,1)S(1)}, u32[]{:S(2)}, u32[]{:S(2)}) collective-permute-start(bf16[4,192,384]{2,1,0:T(8,128)(2,1)} %get-tuple-element.153), channel_id=1, source_target_pairs={{0,8},{2,10},{4,12},{6,14},{8,0},{10,2},{12,4},{14,6},{16,24},{18,... | collective-permute-start | bytes 1769480 | tf_op jit(solution)/shard_map/ppermute | solution.py:361
  163.4 26.0 %collective-permute-start.20 = (bf16[4,48,1536]{2,1,0:T(8,128)(2,1)}, bf16[4,48,1536]{2,1,0:T(8,128)(2,1)S(1)}, u32[]{:S(2)}, u32[]{:S(2)}) collective-permute-start(bf16[4,48,1536]{2,1,0:T(8,128)(2,1)} %get-tuple-element.175), channel_id=1, source_target_pairs={{0,4},{2,6},{4,0},{6,2},{8,12},{10,14},{12,8},{14,10},{16,20},{18,... | collective-permute-start | bytes 1769480 | tf_op jit(solution)/shard_map/ppermute | solution.py:361
  163.9 25.4 %collective-permute-start.21 = (bf16[4,48,1536]{2,1,0:T(8,128)(2,1)}, bf16[4,48,1536]{2,1,0:T(8,128)(2,1)S(1)}, u32[]{:S(2)}, u32[]{:S(2)}) collective-permute-start(bf16[4,48,1536]{2,1,0:T(8,128)(2,1)} %get-tuple-element.176), channel_id=1, source_target_pairs={{0,8},{2,10},{4,12},{6,14},{8,0},{10,2},{12,4},{14,6},{16,24},{18,... | collective-permute-start | bytes 1769480 | tf_op jit(solution)/shard_map/ppermute | solution.py:361
  164.1 14.9 %copy-start.24 = (f32[3,768]{1,0:T(4,128)S(1)}, f32[3,768]{1,0:T(4,128)}, u32[]{:S(2)}) copy-start(f32[3,768]{1,0:T(4,128)} %slice.114) | copy-start | bytes 27652
  164.1 14.9 %copy-start.25 = (f32[3,768]{1,0:T(4,128)S(1)}, f32[3,768]{1,0:T(4,128)}, u32[]{:S(2)}) copy-start(f32[3,768]{1,0:T(4,128)} %slice.113) | copy-start | bytes 27652
  185.9 39.8 %collective-permute-start.28 = (bf16[2,192,384]{2,1,0:T(8,128)(2,1)}, bf16[2,192,384]{2,1,0:T(8,128)(2,1)S(1)}, u32[]{:S(2)}, u32[]{:S(2)}) collective-permute-start(bf16[2,192,384]{2,1,0:T(8,128)(2,1)} %get-tuple-element.185), channel_id=1, source_target_pairs={{0,8},{2,10},{4,12},{6,14},{8,0},{10,2},{12,4},{14,6},{16,24},{18,... | collective-permute-start | bytes 884744 | tf_op jit(solution)/shard_map/ppermute | solution.py:361
  187.8 39.4 %collective-permute-start.29 = (bf16[2,192,384]{2,1,0:T(8,128)(2,1)}, bf16[2,192,384]{2,1,0:T(8,128)(2,1)S(1)}, u32[]{:S(2)}, u32[]{:S(2)}) collective-permute-start(bf16[2,192,384]{2,1,0:T(8,128)(2,1)} %get-tuple-element.186), channel_id=1, source_target_pairs={{0,4},{2,6},{4,0},{6,2},{8,12},{10,14},{12,8},{14,10},{16,20},{18,... | collective-permute-start | bytes 884744 | tf_op jit(solution)/shard_map/ppermute | solution.py:361
  194.3 16.3 %collective-permute-start.22 = (bf16[2,48,1536]{2,1,0:T(8,128)(2,1)}, bf16[2,48,1536]{2,1,0:T(8,128)(2,1)S(1)}, u32[]{:S(2)}, u32[]{:S(2)}) collective-permute-start(bf16[2,48,1536]{2,1,0:T(8,128)(2,1)} %get-tuple-element.178), channel_id=1, source_target_pairs={{0,8},{2,10},{4,12},{6,14},{8,0},{10,2},{12,4},{14,6},{16,24},{18,... | collective-permute-start | bytes 884744 | tf_op jit(solution)/shard_map/ppermute | solution.py:361
  194.8 15.8 %collective-permute-start.23 = (bf16[2,48,1536]{2,1,0:T(8,128)(2,1)}, bf16[2,48,1536]{2,1,0:T(8,128)(2,1)S(1)}, u32[]{:S(2)}, u32[]{:S(2)}) collective-permute-start(bf16[2,48,1536]{2,1,0:T(8,128)(2,1)} %get-tuple-element.180), channel_id=1, source_target_pairs={{0,4},{2,6},{4,0},{6,2},{8,12},{10,14},{12,8},{14,10},{16,20},{18,... | collective-permute-start | bytes 884744 | tf_op jit(solution)/shard_map/ppermute | solution.py:361
  210.6 63.7 %collective-permute-start.9 = (bf16[8,48,3328]{2,1,0:T(8,128)(2,1)}, bf16[8,48,3328]{2,1,0:T(8,128)(2,1)S(1)}, u32[]{:S(2)}, u32[]{:S(2)}) collective-permute-start(bf16[8,48,3328]{2,1,0:T(8,128)(2,1)} %get-tuple-element.157), channel_id=1, source_target_pairs={{0,2},{2,0},{4,6},{6,4},{8,10},{10,8},{12,14},{14,12},{16,18},{18,... | collective-permute-start | bytes 7667720 | tf_op jit(solution)/shard_map/ppermute | solution.py:361
  214.2 16.6 %collective-permute-start.24 = (bf16[1,48,1536]{2,1,0:T(8,128)(2,1)}, bf16[1,48,1536]{2,1,0:T(8,128)(2,1)S(1)}, u32[]{:S(2)}, u32[]{:S(2)}) collective-permute-start(bf16[1,48,1536]{2,1,0:T(8,128)(2,1)} %get-tuple-element.182), channel_id=1, source_target_pairs={{0,16},{2,18},{4,20},{6,22},{8,24},{10,26},{12,28},{14,30},{16,0},... | collective-permute-start | bytes 442376 | tf_op jit(solution)/shard_map/ppermute | solution.py:361
  225.7 19.2 %copy-start.37 = (bf16[1,48,1536]{2,1,0:T(8,128)(2,1)S(1)}, bf16[1,48,1536]{2,1,0:T(8,128)(2,1)}, u32[]{:S(2)}) copy-start(bf16[1,48,1536]{2,1,0:T(8,128)(2,1)} %get-tuple-element.184) | copy-start | bytes 442372
  225.7 91.1 %collective-permute-start.10 = (bf16[512,768]{1,0:T(8,128)(2,1)}, bf16[512,768]{1,0:T(8,128)(2,1)}, u32[]{:S(2)}, u32[]{:S(2)}) collective-permute-start(bf16[512,768]{1,0:T(8,128)(2,1)} %get-tuple-element.162), channel_id=1, source_target_pairs={{0,1},{1,0},{2,3},{3,2},{4,5},{5,4},{6,7},{7,6},{8,9},{9,8},{10,11... | collective-permute-start | bytes 2359304 | tf_op jit(solution)/shard_map/ppermute | solution.py:361
  225.7 31.2 %copy-start.22 = (bf16[1,48,1536]{2,1,0:T(8,128)(2,1)S(1)}, bf16[1,48,1536]{2,1,0:T(8,128)(2,1)}, u32[]{:S(2)}) copy-start(bf16[1,48,1536]{2,1,0:T(8,128)(2,1)} %get-tuple-element.183) | copy-start | bytes 442372
  225.8 78.3 %collective-permute-start.11 = (bf16[512,768]{1,0:T(8,128)(2,1)}, bf16[512,768]{1,0:T(8,128)(2,1)}, u32[]{:S(2)}, u32[]{:S(2)}) collective-permute-start(bf16[512,768]{1,0:T(8,128)(2,1)} %get-tuple-element.164), channel_id=1, source_target_pairs={{1,0},{3,2},{5,4},{7,6},{9,8},{11,10},{13,12},{15,14},{17,16},{19,... | collective-permute-start | bytes 2359304 | tf_op jit(solution)/shard_map/ppermute | solution.py:697
  230.8 14.1 %collective-permute-start.30 = (bf16[1,192,384]{2,1,0:T(8,128)(2,1)}, bf16[1,192,384]{2,1,0:T(8,128)(2,1)S(1)}, u32[]{:S(2)}, u32[]{:S(2)}) collective-permute-start(bf16[1,192,384]{2,1,0:T(8,128)(2,1)} %get-tuple-element.188), channel_id=1, source_target_pairs={{0,16},{2,18},{4,20},{6,22},{8,24},{10,26},{12,28},{14,30},{16,0},... | collective-permute-start | bytes 442376 | tf_op jit(solution)/shard_map/ppermute | solution.py:361
  230.8 26.2 %collective-permute-start.32 = (bf16[1,192,384]{2,1,0:T(8,128)(2,1)}, bf16[1,192,384]{2,1,0:T(8,128)(2,1)S(1)}, u32[]{:S(2)}, u32[]{:S(2)}) collective-permute-start(bf16[1,192,384]{2,1,0:T(8,128)(2,1)} %get-tuple-element.190), channel_id=1, source_target_pairs={{0,16},{2,18},{4,20},{6,22},{8,24},{10,26},{12,28},{14,30},{16,0},... | collective-permute-start | bytes 442376 | tf_op jit(solution)/shard_map/ppermute | solution.py:361
  244.9 8.8 %collective-permute-start.26 = (bf16[1,48,1536]{2,1,0:T(8,128)(2,1)S(1)}, bf16[1,48,1536]{2,1,0:T(8,128)(2,1)S(1)}, u32[]{:S(2)}, u32[]{:S(2)}) collective-permute-start(bf16[1,48,1536]{2,1,0:T(8,128)(2,1)S(1)} %copy-done.37), channel_id=1, source_target_pairs={{0,16},{2,18},{4,20},{6,22},{8,24},{10,26},{12,28},{14,30},{16,0},... | collective-permute-start | bytes 442376 | tf_op jit(solution)/shard_map/ppermute | solution.py:361
  253.6 20.6 %collective-permute-start.31 = (bf16[192,384]{1,0:T(8,128)(2,1)S(1)}, bf16[192,384]{1,0:T(8,128)(2,1)S(1)}, u32[]{:S(2)}, u32[]{:S(2)}) collective-permute-start(bf16[192,384]{1,0:T(8,128)(2,1)S(1)} %fusion.6), channel_id=1, source_target_pairs={{0,1},{1,0},{2,3},{3,2},{4,5},{5,4},{6,7},{7,6},{8,9},{9,8},{10,11... | collective-permute-start | bytes 442376 | tf_op jit(solution)/shard_map/ppermute | solution.py:361
  257.0 11.8 %collective-permute-start.25 = (bf16[48,1536]{1,0:T(8,128)(2,1)S(1)}, bf16[48,1536]{1,0:T(8,128)(2,1)S(1)}, u32[]{:S(2)}, u32[]{:S(2)}) collective-permute-start(bf16[48,1536]{1,0:T(8,128)(2,1)S(1)} %fusion.4), channel_id=1, source_target_pairs={{0,1},{1,0},{2,3},{3,2},{4,5},{5,4},{6,7},{7,6},{8,9},{9,8},{10,11... | collective-permute-start | bytes 442376 | tf_op jit(solution)/shard_map/ppermute | solution.py:361
  268.8 5.1 %collective-permute-start.27 = (bf16[48,1536]{1,0:T(8,128)(2,1)S(1)}, bf16[48,1536]{1,0:T(8,128)(2,1)S(1)}, u32[]{:S(2)}, u32[]{:S(2)}) collective-permute-start(bf16[48,1536]{1,0:T(8,128)(2,1)S(1)} %fusion.5), channel_id=1, source_target_pairs={{0,1},{1,0},{2,3},{3,2},{4,5},{5,4},{6,7},{7,6},{8,9},{9,8},{10,11... | collective-permute-start | bytes 442376 | tf_op jit(solution)/shard_map/ppermute | solution.py:361
  273.9 10.5 %collective-permute-start.33 = (bf16[192,384]{1,0:T(8,128)(2,1)S(1)}, bf16[192,384]{1,0:T(8,128)(2,1)S(1)}, u32[]{:S(2)}, u32[]{:S(2)}) collective-permute-start(bf16[192,384]{1,0:T(8,128)(2,1)S(1)} %fusion.7), channel_id=1, source_target_pairs={{0,1},{1,0},{2,3},{3,2},{4,5},{5,4},{6,7},{7,6},{8,9},{9,8},{10,11... | collective-permute-start | bytes 442376 | tf_op jit(solution)/shard_map/ppermute | solution.py:361
  281.2 15.1 %collective-permute-start.12 = (bf16[4,48,1664]{2,1,0:T(8,128)(2,1)}, bf16[4,48,1664]{2,1,0:T(8,128)(2,1)S(1)}, u32[]{:S(2)}, u32[]{:S(2)}) collective-permute-start(bf16[4,48,1664]{2,1,0:T(8,128)(2,1)} %get-tuple-element.165), channel_id=1, source_target_pairs={{0,4},{2,6},{4,0},{6,2},{8,12},{10,14},{12,8},{14,10},{16,20},{18,... | collective-permute-start | bytes 1916936 | tf_op jit(solution)/shard_map/ppermute | solution.py:361
  282.8 14.7 %collective-permute-start.13 = (bf16[4,48,1664]{2,1,0:T(8,128)(2,1)}, bf16[4,48,1664]{2,1,0:T(8,128)(2,1)S(1)}, u32[]{:S(2)}, u32[]{:S(2)}) collective-permute-start(bf16[4,48,1664]{2,1,0:T(8,128)(2,1)} %get-tuple-element.166), channel_id=1, source_target_pairs={{0,8},{2,10},{4,12},{6,14},{8,0},{10,2},{12,4},{14,6},{16,24},{18,... | collective-permute-start | bytes 1916936 | tf_op jit(solution)/shard_map/ppermute | solution.py:361
  301.9 10.7 %collective-permute-start.14 = (bf16[2,48,1664]{2,1,0:T(8,128)(2,1)}, bf16[2,48,1664]{2,1,0:T(8,128)(2,1)S(1)}, u32[]{:S(2)}, u32[]{:S(2)}) collective-permute-start(bf16[2,48,1664]{2,1,0:T(8,128)(2,1)} %get-tuple-element.168), channel_id=1, source_target_pairs={{0,8},{2,10},{4,12},{6,14},{8,0},{10,2},{12,4},{14,6},{16,24},{18,... | collective-permute-start | bytes 958472 | tf_op jit(solution)/shard_map/ppermute | solution.py:361
  303.5 9.1 %collective-permute-start.15 = (bf16[2,48,1664]{2,1,0:T(8,128)(2,1)}, bf16[2,48,1664]{2,1,0:T(8,128)(2,1)S(1)}, u32[]{:S(2)}, u32[]{:S(2)}) collective-permute-start(bf16[2,48,1664]{2,1,0:T(8,128)(2,1)} %get-tuple-element.170), channel_id=1, source_target_pairs={{0,4},{2,6},{4,0},{6,2},{8,12},{10,14},{12,8},{14,10},{16,20},{18,... | collective-permute-start | bytes 958472 | tf_op jit(solution)/shard_map/ppermute | solution.py:361
  316.4 12.3 %collective-permute-start.18 = (bf16[1,48,1664]{2,1,0:T(8,128)(2,1)}, bf16[1,48,1664]{2,1,0:T(8,128)(2,1)S(1)}, u32[]{:S(2)}, u32[]{:S(2)}) collective-permute-start(bf16[1,48,1664]{2,1,0:T(8,128)(2,1)} %get-tuple-element.174), channel_id=1, source_target_pairs={{0,16},{2,18},{4,20},{6,22},{8,24},{10,26},{12,28},{14,30},{16,0},... | collective-permute-start | bytes 479240 | tf_op jit(solution)/shard_map/ppermute | solution.py:361
  318.1 10.6 %copy-start.21 = (bf16[1,48,1664]{2,1,0:T(8,128)(2,1)S(1)}, bf16[1,48,1664]{2,1,0:T(8,128)(2,1)}, u32[]{:S(2)}) copy-start(bf16[1,48,1664]{2,1,0:T(8,128)(2,1)} %get-tuple-element.173) | copy-start | bytes 479236
  318.1 12.6 %copy-start.20 = (bf16[1,48,1664]{2,1,0:T(8,128)(2,1)S(1)}, bf16[1,48,1664]{2,1,0:T(8,128)(2,1)}, u32[]{:S(2)}) copy-start(bf16[1,48,1664]{2,1,0:T(8,128)(2,1)} %get-tuple-element.171) | copy-start | bytes 479236
  319.4 11.3 %collective-permute-start.16 = (bf16[1,48,1664]{2,1,0:T(8,128)(2,1)S(1)}, bf16[1,48,1664]{2,1,0:T(8,128)(2,1)S(1)}, u32[]{:S(2)}, u32[]{:S(2)}) collective-permute-start(bf16[1,48,1664]{2,1,0:T(8,128)(2,1)S(1)} %copy-done.36), channel_id=1, source_target_pairs={{0,16},{2,18},{4,20},{6,22},{8,24},{10,26},{12,28},{14,30},{16,0},... | collective-permute-start | bytes 479240 | tf_op jit(solution)/shard_map/ppermute | solution.py:361
  328.8 6.8 %collective-permute-start.19 = (bf16[48,1664]{1,0:T(8,128)(2,1)S(1)}, bf16[48,1664]{1,0:T(8,128)(2,1)S(1)}, u32[]{:S(2)}, u32[]{:S(2)}) collective-permute-start(bf16[48,1664]{1,0:T(8,128)(2,1)S(1)} %fusion.3), channel_id=1, source_target_pairs={{0,1},{1,0},{2,3},{3,2},{4,5},{5,4},{6,7},{7,6},{8,9},{9,8},{10,11... | collective-permute-start | bytes 479240 | tf_op jit(solution)/shard_map/ppermute | solution.py:361
  330.8 6.5 %collective-permute-start.17 = (bf16[48,1664]{1,0:T(8,128)(2,1)S(1)}, bf16[48,1664]{1,0:T(8,128)(2,1)S(1)}, u32[]{:S(2)}, u32[]{:S(2)}) collective-permute-start(bf16[48,1664]{1,0:T(8,128)(2,1)S(1)} %fusion.2), channel_id=1, source_target_pairs={{0,1},{1,0},{2,3},{3,2},{4,5},{5,4},{6,7},{7,6},{8,9},{9,8},{10,11... | collective-permute-start | bytes 479240 | tf_op jit(solution)/shard_map/ppermute | solution.py:361
  (24 other events, 77.6 us)

commit v2 on v1

v2 whole, which is shorter than its diff:
```python
import functools
import math

import jax
import jax.numpy as jnp
from jax import lax
from jax.experimental import pallas as pl
from jax.experimental.pallas import tpu as pltpu
from jax.sharding import PartitionSpec as P

EPSILON = 1e-05
BF = jnp.bfloat16
F32 = jnp.float32
MIB = 1024 * 1024
NEGATIVE = -1e30

SIDE, CORE, LIVE, OWNER, SOURCE = 0, 1, 2, 4, 5


def dot(a, b, ca=1, cb=0):
    return lax.dot_general(a, b, (((ca,), (cb,)), ((), ())), preferred_element_type=F32)


def params(mebibytes):
    return pltpu.CompilerParams(vmem_limit_bytes=mebibytes * MIB)


def cost(flops, read):
    return pl.CostEstimate(flops=int(flops), bytes_accessed=int(read), transcendentals=0)


def once(shape, index):
    return pl.BlockSpec(shape, index, pipeline_mode=pl.Buffered(1))


def mask_columns(mask_row):
    penalty = jnp.where(mask_row == 0, NEGATIVE, 0.0).astype(F32)
    return jnp.broadcast_to(penalty, (128, penalty.shape[1])).T


def project_own(meta, tok, mask, w, vec, q_t, k, v_t, mb):
    step = pl.program_id(0)
    rows = tok[...]

    @pl.when(step == 0)
    def _():
        queries = (dot(rows, w[...]) + vec[0:1, :]).astype(BF)
        q_t[...] = (queries * 0.125).T
        mb[...] = mask_columns(mask[...])

    @pl.when(step == 1)
    def _():
        k[...] = dot(rows, w[...]).astype(BF)

    @pl.when(step == 2)
    def _():
        v_t[...] = (dot(rows, w[...]) + vec[1:2, :]).astype(BF).T


def pad_pair(part, half):
    zeros = jnp.zeros_like(part)
    return jnp.concatenate([part, zeros] if half == 0 else [zeros, part], axis=0)


def units(heads, size, total, meta):
    pair = pl.program_id(0)
    out = []
    for half in range(2):
        for slot, queries in enumerate((slice(0, size), slice(size, total))):
            source = meta[SOURCE + slot * heads + 2 * pair + half]
            out.append((half, slice(64 * half, 64 * half + 64), queries, source))
    return out


def project_others(meta, vec, masks, starts, ins, k, v_t, q_t, mb, w, two, came):
    size, width = two.shape
    half_rows = size // 2
    own_two, partner_two = starts
    later = ins
    for copy in later:
        copy.start()

    @pl.when(meta[SIDE] == 0)
    def _():
        own_two.start()

    @pl.when(meta[SIDE] == 1)
    def _():
        partner_two.start()

    mb[1] = mask_columns(masks[0:1, :])
    mb[2] = mask_columns(masks[1:2, :])
    own_two.wait()
    later[0].wait()
    k[1] = dot(two[...], w[:, width : 2 * width]).astype(BF)
    later[1].wait()
    k[2] = dot(came[...], w[:, width : 2 * width]).astype(BF)
    later[2].wait()
    v_t[1] = (dot(two[...], w[:, 2 * width :]) + vec[1:2, :]).astype(BF).T
    v_t[2] = (dot(came[...], w[:, 2 * width :]) + vec[1:2, :]).astype(BF).T
    later[3].wait()
    rows = two[pl.ds(pl.multiple_of(meta[SIDE] * half_rows, half_rows), half_rows), :]
    q_t[:, size:] = ((dot(rows, w[:, :width]) + vec[0:1, :]).astype(BF) * 0.125).T
    for copy in later[4:]:
        copy.wait()


def attention_forward(
    heads, meta, masks, vec, tok_in, came_in, w_in, q_own, k_own, v_own, mb_own,
    probs, att, att_t, inv, q_out, k_out, v_out, two_out,
    q_t, k, v_t, mb, w, two, came, sems, out_sems,
):
    size, total = k.shape[1], q_t.shape[1]
    width = k.shape[2]
    step = pl.program_id(0)
    copy = pltpu.make_async_copy
    outs = [
        copy(source, target, out_sems.at[at])
        for at, (source, target) in enumerate(((q_t, q_out), (k, k_out), (v_t, v_out), (two, two_out)))
    ]

    @pl.when(step == 0)
    def _():
        columns = [slice(width, 2 * width), slice(2 * width, 3 * width), slice(0, width)]
        starts = [copy(tok_in.at[1], two, sems.at[0]), copy(came_in.at[1], two, sems.at[0])]
        ins = [
            copy(w_in.at[:, columns[0]], w.at[:, columns[0]], sems.at[1]),
            copy(came_in.at[0], came, sems.at[2]),
            copy(w_in.at[:, columns[1]], w.at[:, columns[1]], sems.at[3]),
            copy(w_in.at[:, columns[2]], w.at[:, columns[2]], sems.at[4]),
            copy(q_own, q_t.at[:, pl.ds(0, size)], sems.at[5]),
            copy(k_own, k.at[0], sems.at[6]),
            copy(v_own, v_t.at[0], sems.at[7]),
            copy(mb_own, mb.at[0], sems.at[8]),
        ]
        project_others(meta, vec, masks, starts, ins, k, v_t, q_t, mb, w, two, came)
        for out in outs:
            out.start()

    todo = units(heads, size, total, meta)
    lanes = pl.ds(pl.multiple_of(step * 128, 128), 128)

    def rows_of(span):
        return pl.ds(pl.multiple_of(step * 128 + span.start, 64), 64)

    def score(unit):
        half, span, queries, source = unit
        return dot(k[source, :, lanes], pad_pair(q_t[rows_of(span), queries], half))

    def soften(unit, scores):
        half, span, queries, source = unit
        scores = scores + jnp.concatenate([mb[source]] * (scores.shape[1] // 128), axis=1)
        weights = jnp.exp(scores - jnp.max(scores, axis=0, keepdims=True))
        inverse = 1.0 / jnp.sum(weights, axis=0, keepdims=True)
        low = weights.astype(BF)
        probs[half, :, queries] = low
        inv[0, half : half + 1, queries] = inverse
        return low, inverse

    def attend(unit, soft):
        half, span, queries, source = unit
        att_t[span, queries] = (dot(v_t[source, rows_of(span), :], soft[0]) * soft[1]).astype(BF)

    scores = {0: score(todo[0])}
    soft = {}
    for at in range(len(todo) + 1):
        if at + 1 < len(todo):
            scores[at + 1] = score(todo[at + 1])
        if at < len(todo):
            soft[at] = soften(todo[at], scores.pop(at))
        if at > 0:
            attend(todo[at - 1], soft.pop(at - 1))
    att[...] = att_t[...].T

    @pl.when(step == pl.num_programs(0) - 1)
    def _():
        for out in outs:
            out.wait()


def lane_sums(block):
    width = block.shape[1]
    part = block[:, :128]
    for at in range(128, width, 128):
        part = part + block[:, at : at + 128]
    return jnp.sum(part.T, axis=0, keepdims=True)


def attention_backward(
    heads, meta, probs, k, v_t, q_t, do_t, att_t, inv, gq_t, gkv_t, bq, bv, sum_k, sum_v, sum_q, k_t, v
):
    size, total = k.shape[1], q_t.shape[1]
    for at in range(3):
        k_t[at] = k[at].T
        v[at] = v_t[at].T
    todo = units(heads, size, total, meta)
    sum_k[...] = jnp.zeros_like(sum_k)
    sum_v[...] = jnp.zeros_like(sum_v)

    def begin(unit):
        half, span, queries, source = unit
        scaled = do_t[span, queries].astype(F32) * inv[0, half : half + 1, queries]
        delta = jnp.sum(scaled * att_t[span, queries].astype(F32), axis=0, keepdims=True)
        scaled = scaled.astype(BF)
        return scaled, delta, dot(v[source], pad_pair(scaled, half))

    def middle(unit, begun):
        half, span, queries, source = unit
        scaled, delta, grad_probs = begun
        low = probs[half, :, queries]
        sum_v[source, span, :] += dot(scaled, low, 1, 1)
        return (low.astype(F32) * (grad_probs - delta)).astype(BF)

    def end(unit, grad_scores):
        half, span, queries, source = unit
        sum_k[source, span, :] += dot(q_t[span, queries], grad_scores, 1, 1)
        grad_q = dot(k_t[source, span, :], grad_scores) * 0.125
        sum_q[span, queries] = grad_q
        gq_t[span, queries] = grad_q.astype(BF)

    begun = {0: begin(todo[0])}
    grads = {}
    for at in range(len(todo) + 1):
        if at + 1 < len(todo):
            begun[at + 1] = begin(todo[at + 1])
        if at < len(todo):
            grads[at] = middle(todo[at], begun.pop(at))
        if at > 0:
            end(todo[at - 1], grads.pop(at - 1))
    gkv_t[:, 0] = sum_k[...].astype(BF)
    gkv_t[:, 1] = sum_v[...].astype(BF)
    bq[...] = lane_sums(sum_q[...])
    bv[...] = lane_sums(sum_v[0] + sum_v[1] + sum_v[2])


def normalise(rows):
    centred = rows - jnp.mean(rows, axis=-1, keepdims=True)
    scale = lax.rsqrt(jnp.mean(centred * centred, axis=-1, keepdims=True) + EPSILON)
    return centred * scale, scale


def norm_backward(grad, norm, scale, gain):
    scaled = grad * gain
    mean = jnp.mean(scaled, axis=-1, keepdims=True)
    along = jnp.mean(scaled * norm, axis=-1, keepdims=True)
    return scale * (scaled - mean - norm * along)


def gelu_pair(u):
    below = 0.5 + 0.5 * lax.erf(u * math.sqrt(0.5))
    bell = jnp.exp2((-0.5 * math.log2(math.e)) * (u * u)) * (1.0 / math.sqrt(2.0 * math.pi))
    return u * below, below + u * bell


B_OUT, GAIN_ONE, SHIFT_ONE, B_BACK, GAIN_TWO, SHIFT_TWO = 2, 3, 4, 5, 6, 7


def tiles_of(total, tile):
    return [slice(at, at + tile) for at in range(0, total, tile)]


def split_cores(meta, block, keep, send, groups, rows):
    mine = meta[CORE]
    for at in range(groups):
        low = block[2 * at * rows : (2 * at + 1) * rows]
        high = block[(2 * at + 1) * rows : (2 * at + 2) * rows]
        if keep is not None:
            keep[at] = jnp.where(mine == 0, low, high).astype(BF)
        if send is not None:
            send[at] = jnp.where(mine == 0, high, low).astype(BF)


def rows_forward(
    steps, meta, tok, two_half, att, cot, cot_half, cot_came, w_out, vec, w_in, b_in, w_back,
    slope, keep, send, sums, first_out, normed_out, mixed_out, mixed_two_out, second_out, back_out,
    first, normed_low, mixed, second, back_low, active, sems,
):
    step = pl.program_id(0)
    total = att.shape[0]
    tile = two_half.shape[0]
    size = total - tile
    chunk = w_in.shape[1]
    tiles = tiles_of(total, tile)
    copies = [
        pltpu.make_async_copy(source, target, sems.at[at])
        for at, (source, target) in enumerate(
            (
                (first, first_out), (normed_low, normed_out), (mixed.at[pl.ds(0, size)], mixed_out),
                (mixed.at[pl.ds(size, tile)], mixed_two_out), (second, second_out), (back_low, back_out),
            )
        )
    ]

    @pl.when(step == 0)
    def _():
        for at, span in enumerate(tiles):
            rows = (tok[span, :] if at + 1 < len(tiles) else two_half[...]).astype(F32)
            rows = rows + dot(att[span, :], w_out[...]) + vec[B_OUT : B_OUT + 1, :]
            first[span, :] = rows
            result = normalise(rows)[0] * vec[GAIN_ONE : GAIN_ONE + 1, :] + vec[SHIFT_ONE : SHIFT_ONE + 1, :]
            normed_low[span, :] = result.astype(BF)
            second[span, :] = result + vec[B_BACK : B_BACK + 1, :]
        copies[0].start()
        copies[1].start()

    @pl.when(step < steps)
    def _():
        hidden = dot(normed_low[...], w_in[...]) + b_in[...]
        value, grad = gelu_pair(hidden)
        value = value.astype(BF)
        active[:, pl.ds(pl.multiple_of(step * chunk, chunk), chunk)] = value
        slope[...] = grad.astype(BF)
        second[...] += dot(value, w_back[...])

    @pl.when(step == steps - 1)
    def _():
        sums[...] = jnp.zeros_like(sums)
        gain, shift = vec[GAIN_TWO : GAIN_TWO + 1, :], vec[SHIFT_TWO : SHIFT_TWO + 1, :]
        for at, span in enumerate(tiles):
            last = at + 1 == len(tiles)
            live = meta[LIVE + last].astype(F32)
            norm, scale = normalise(second[span, :])
            mixed[span, :] = ((norm * gain + shift) * live).astype(BF)
            cotangent = jnp.where(meta[SIDE] == 0, cot_half[...], cot_came[...]) if last else cot[span, :]
            grad = cotangent.astype(F32) * live
            sums[0:1, :] += jnp.sum(grad * norm, axis=0, keepdims=True)
            sums[1:2, :] += jnp.sum(grad, axis=0, keepdims=True)
            grad = norm_backward(grad, norm, scale, gain)
            sums[2:3, :] += jnp.sum(grad, axis=0, keepdims=True)
            second[span, :] = grad
            back_low[span, :] = grad.astype(BF)
        for copy in copies[2:]:
            copy.start()

    @pl.when(step >= steps)
    def _():
        groups, rows, _ = keep.shape
        columns = 2 * groups * rows
        part = active[:, pl.ds(pl.multiple_of((step - steps) * columns, columns), columns)]
        split_cores(meta, dot(part, back_low[...], 0, 0), keep, send, groups, rows)

    @pl.when(step == pl.num_programs(0) - 1)
    def _():
        for copy in copies:
            copy.wait()


def rows_backward(
    meta, back_low, normed_low, slope, w_in, w_back, w_out, vec, first_in, second_in, att_in,
    keep, *refs
):
    sends, (g_first, first_low, do_t, b_in, sums, first, g_normed, g_second, att_t, sems) = refs[:-10], refs[-10:]
    step = pl.program_id(0)
    last = pl.num_programs(0) - 1
    total = back_low.shape[0]
    tiles = tiles_of(total, total // 3)
    copies = [
        pltpu.make_async_copy(first_in, first, sems.at[0]),
        pltpu.make_async_copy(second_in, g_second, sems.at[1]),
        pltpu.make_async_copy(att_in, att_t, sems.at[2]),
    ]

    @pl.when(step == 0)
    def _():
        for copy in copies:
            copy.start()
        g_normed[...] = jnp.zeros_like(g_normed)

    @pl.when(step < last)
    def _():
        grad = dot(back_low[...], w_back[...], 1, 1) * slope[...].astype(F32)
        b_in[...] = jnp.sum(grad, axis=0, keepdims=True)
        low = grad.astype(BF)
        g_normed[...] += dot(low, w_in[...], 1, 1)
        block = dot(normed_low[...], low, 0, 0)
        for number, send in enumerate(sends[:-1]):

            @pl.when(step == number)
            def _():
                split_cores(meta, block, None, send, keep.shape[0], keep.shape[1])

        split_cores(meta, block, keep, None, keep.shape[0], keep.shape[1])

    @pl.when(step == last)
    def _():
        for copy in copies:
            copy.wait()
        sums[...] = jnp.zeros_like(sums)
        for span in tiles:
            norm, scale = normalise(first[span, :])
            grad = g_normed[span, :] + g_second[span, :]
            sums[0:1, :] += jnp.sum(grad * norm, axis=0, keepdims=True)
            sums[1:2, :] += jnp.sum(grad, axis=0, keepdims=True)
            grad = norm_backward(grad, norm, scale, vec[GAIN_ONE : GAIN_ONE + 1, :])
            sums[2:3, :] += jnp.sum(grad, axis=0, keepdims=True)
            g_first[span, :] = grad
            first_low[span, :] = grad.astype(BF)
        do_t[...] = dot(w_out[...], first_low[...], 1, 1).astype(BF)
        split_cores(meta, dot(att_t[...], first_low[...]), keep, sends[-1], keep.shape[0], keep.shape[1])


def weight_gradients(
    meta, tok_in, two_in, other_in, gq_in, gkv_in, sums_two, sums_one, g_bq, g_bv, g_b_in,
    keep_out, send_out,
    tok, gq_t, gkv_t, tok_t, keep, send, keep_last, send_last, sems, out_sems,
):
    _, size, width = tok.shape
    half_rows = size // 2
    ins = [
        pltpu.make_async_copy(source, target, sems.at[at])
        for at, (source, target) in enumerate(
            [
                (tok_in.at[0], tok.at[0]), (two_in, tok.at[1]), (gq_in, gq_t), (other_in.at[0], tok.at[2]),
                (gkv_in.at[0], gkv_t.at[0]), (gkv_in.at[1], gkv_t.at[1]), (gkv_in.at[2], gkv_t.at[2]),
            ]
        )
    ]
    for copy in ins:
        copy.start()
    groups, own_rows = keep.shape[1], keep.shape[2]

    def outs(section):
        slot = section % 2
        columns = pl.ds(section * width, width)
        return [
            pltpu.make_async_copy(keep.at[slot], keep_out.at[:, :, columns], out_sems.at[2 * slot]),
            pltpu.make_async_copy(send.at[slot], send_out.at[:, :, columns], out_sems.at[2 * slot + 1]),
        ]

    def finish(section, block):
        slot = section % 2
        if section >= 2:
            for copy in outs(section - 2):
                copy.wait()
        split_cores(meta, block, keep.at[slot], send.at[slot], groups, own_rows)
        for copy in outs(section):
            copy.start()

    def turn(at):
        tok_t[:, at * size : (at + 1) * size] = tok[at].T

    vectors = [sums_two[0:3, :], sums_one[0:3, :], g_bq[...], g_bv[...], jnp.zeros((120, width), F32)]
    vectors = jnp.concatenate(vectors, axis=0).T
    per_owner = g_b_in.shape[1] // (2 * groups)
    line = min(64, per_owner)
    bias_rows = []
    for at in range(2 * groups):
        lines = [
            jnp.concatenate(
                [
                    jnp.zeros((1, 64), F32),
                    g_b_in[:, at * per_owner + to : at * per_owner + to + line],
                    jnp.zeros((1, 64 - line), F32),
                ][: 2 + (line < 64)],
                axis=1,
            )
            for to in range(0, per_owner, line)
        ]
        bias_rows.append(jnp.concatenate(lines + [jnp.zeros((own_rows - len(lines), 128), F32)], axis=0))
    split_cores(meta, vectors + jnp.concatenate(bias_rows, axis=0), keep_last, send_last, groups, own_rows)
    last = [
        pltpu.make_async_copy(keep_last, keep_out.at[:, :, pl.ds(3 * width, 128)], out_sems.at[4]),
        pltpu.make_async_copy(send_last, send_out.at[:, :, pl.ds(3 * width, 128)], out_sems.at[5]),
    ]
    for copy in last:
        copy.start()
    for copy in ins[:3]:
        copy.wait()
    turn(0)
    turn(1)
    half = tok_t[:, pl.ds(pl.multiple_of(size + meta[SIDE] * half_rows, half_rows), half_rows)]
    finish(0, dot(tok_t[:, :size], gq_t[:, :size], 1, 1) + dot(half, gq_t[:, size:], 1, 1))
    for copy in ins[3:]:
        copy.wait()
    turn(2)
    for which in range(2):
        span = slice(which * width, (which + 1) * width)
        block = dot(tok_t[:, :size], gkv_t[0, span, :], 1, 1)
        block = block + dot(tok_t[:, size : 2 * size], gkv_t[1, span, :], 1, 1)
        finish(1 + which, block + dot(tok_t[:, 2 * size :], gkv_t[2, span, :], 1, 1))
    for copy in outs(1) + outs(2) + last:
        copy.wait()


def tokens_backward(meta, w, gq_t, gkv_t, g_first, sent, two, own, w_kv, w_q):
    step = pl.program_id(0)
    size, width = own.shape
    half_rows = size // 2

    @pl.when(step == 0)
    def _():
        w_kv[...] = w[:, width:]
        w_q[...] = w[:, :width]
        sent[0] = dot(w_kv[...], gkv_t[...]).T.astype(BF)

    @pl.when(step == 1)
    def _():
        two[...] = dot(w_kv[...], gkv_t[...]).T
        span = pl.ds(pl.multiple_of(meta[SIDE] * half_rows, half_rows), half_rows)
        two[span, :] += dot(w_q[...], gq_t[:, size:]).T + g_first[size:, :]
        sent[1] = two[...].astype(BF)

    @pl.when(step == 2)
    def _():
        total = dot(w_q[...], gq_t[:, :size]) + dot(w_kv[...], gkv_t[...])
        own[...] = total.T + g_first[:size, :]


def flip(value, axis, bit):
    count = lax.axis_size(axis)
    return lax.ppermute(value, axis, [(at, at ^ bit) for at in range(count)])


def after(value, *others):
    return lax.optimization_barrier((value,) + others)[0]


CORE_SUM, QUAD, PAIR = 0, 1, 2


def combine_kernel(plan, meta, *refs):
    refs = list(refs)
    ins = [[refs.pop(0) for _ in range(count)] for _, _, _, count, _ in plan]
    outs = [[refs.pop(0) for _ in range(count)] for _, _, _, _, count in plan]
    for (stage, over_x, bit, _, _), parts, targets in zip(plan, ins, outs):
        if stage == CORE_SUM:
            kept, pieces = parts[0], parts[1:]
            (out,) = targets
            columns = kept.shape[2]
            each = columns // len(pieces)
            for at in range(kept.shape[0]):
                for number, piece in enumerate(pieces):
                    if not over_x:
                        span = slice(each * number, each * (number + 1))
                        total = kept[at, :, span].astype(F32) + piece[at].astype(F32)
                        out[at % 4, at // 4, :, span] = total.astype(BF)
                        continue
                    for side in range(2):
                        low = max(each * number, side * columns // 2)
                        high = min(each * (number + 1), (side + 1) * columns // 2)
                        if low < high:
                            total = kept[at, :, low:high].astype(F32)
                            total = total + piece[at, :, low - each * number : high - each * number].astype(F32)
                            to = slice(low - side * columns // 2, high - side * columns // 2)
                            out[2 * (at % 2) + side, at // 2, :, to] = total.astype(BF)
            continue

        def total_at(index):
            if stage == QUAD:
                (came,) = parts
                return (came[0, index].astype(F32) + came[1, index].astype(F32)) + (
                    came[2, index].astype(F32) + came[3, index].astype(F32)
                )
            kept, came = parts
            return kept[index].astype(F32) + came[index].astype(F32)

        if len(targets) == 1:
            targets[0][...] = total_at(0).astype(BF)
        else:
            mine = (meta[OWNER] >> bit) & 1
            for flipped, out in enumerate(targets):
                which = 1 - mine if flipped else mine
                for to in range(out.shape[0]):
                    out[to] = total_at(2 * to + which).astype(BF)


class Piece:
    def __init__(self, keep, sends, over_x):
        self.over_x = over_x
        self.rows = keep.shape[1]
        self.columns = keep.shape[2] // 2 if over_x else keep.shape[2]
        bits = list(range(1, lax.axis_size("batch").bit_length() - 1))
        self.plane, self.bits = (bits[:1], bits[1:]) if over_x else (bits[:2], bits[2:])
        self.stage = CORE_SUM
        self.parts = [keep] + [flip(send, "batch", 1) for send in sends]

    def shapes(self):
        sds = lambda *lead: jax.ShapeDtypeStruct(lead + (self.rows, self.columns), BF)
        if self.stage == CORE_SUM:
            return [sds(4, self.parts[0].shape[0] // 2 ** len(self.plane))]
        count = self.parts[0].shape[-3]
        return [sds(count // 2)] * 2 if count > 1 else [sds()]

    def taken(self, results):
        self.sending = results[-1]
        if self.stage == CORE_SUM:
            owners = lax.axis_size("batch")
            if self.over_x:
                groups = [
                    [2 * (high + 2 * bit + core) + side for bit in range(2) for side in range(2)]
                    for high in range(0, owners, 4)
                    for core in range(2)
                ]
                came = lax.all_to_all(results[0], ("batch", "blk"), 0, 0, axis_index_groups=groups)
            else:
                groups = [
                    [high + 2 * place + core for place in range(4)] for high in range(0, owners, 8) for core in range(2)
                ]
                came = lax.all_to_all(results[0], "batch", 0, 0, axis_index_groups=groups)
            self.parts = [came]
            self.stage = QUAD
        elif len(results) == 2:
            self.parts = [results[0], flip(results[1], "batch", 1 << self.bits.pop(0))]
            self.stage = PAIR
        else:
            self.parts = [results[0], flip(results[0], "blk", 1)]
            self.stage = None

    def finish(self, side):
        own, came = self.parts
        if not self.over_x:
            return own.astype(F32) + came.astype(F32)
        return jnp.concatenate([jnp.where(side == 0, own, came), jnp.where(side == 0, came, own)], axis=1).astype(F32)


def take(meta, pieces, *order_after):
    operands, plan, shapes = [], [], []
    for piece in pieces:
        piece.parts = list(lax.optimization_barrier(tuple(piece.parts) + order_after)[: len(piece.parts)])
        made = piece.shapes()
        bit = piece.bits[0] if piece.bits else 0
        plan.append((piece.stage, piece.over_x, bit, len(piece.parts), len(made)))
        operands += piece.parts
        shapes += made
    vmem = pl.BlockSpec(memory_space=pltpu.VMEM)
    out = pl.pallas_call(
        functools.partial(combine_kernel, plan),
        in_specs=[pl.BlockSpec(memory_space=pltpu.SMEM)] + [vmem] * len(operands),
        out_specs=[vmem] * len(shapes),
        out_shape=shapes,
        compiler_params=params(28),
        cost_estimate=cost(1, 1),
        name="combine",
    )(meta, *operands)
    for piece, (_, _, _, _, count) in zip(pieces, plan):
        piece.taken(out[:count])
        out = out[count:]
    return tuple(part for piece in pieces for part in piece.parts[:1] if piece.stage != QUAD)


def local(
    tokens, cotangent, counts, perms, key_mask, w_qkv, bias_q, bias_v, w_out, bias_out, gain_one, shift_one,
    w_in, bias_in, w_back, bias_back, gain_two, shift_two,
):
    _, _, size, width = tokens.shape
    heads = perms.shape[1]
    pairs = heads // 2
    hidden = w_in.shape[1]
    half_rows = size // 2
    total = size + half_rows
    owners = lax.axis_size("batch")
    side = lax.axis_index("blk").astype(jnp.int32)
    owner = lax.axis_index("batch").astype(jnp.int32)
    whole = lambda *shape: once(shape, lambda *_: (0,) * len(shape))
    sds = jax.ShapeDtypeStruct
    anywhere = pl.BlockSpec(memory_space=pl.ANY)

    tok = tokens[0]
    came = flip(tok, "blk", 1)

    count = counts[0]
    lookup = jnp.where(count == 2, perms[0], perms[1])
    own = jnp.where(side == 0, lookup[:, 0], lookup[:, 1])
    two = jnp.where(count > 2, lookup[:, 2], 2)
    source = jnp.concatenate([own, two])
    place = jnp.where(source == 2, 1, jnp.where(source == side, 0, 2))
    live = jnp.stack([(side < count).astype(jnp.int32), (count > 2).astype(jnp.int32)])
    meta = jnp.concatenate([jnp.stack([side, owner & 1]), live, owner[None], place])
    vec = jnp.concatenate([bias_q, bias_v, bias_out, gain_one, shift_one, bias_back, gain_two, shift_two]).reshape(8, width)
    own_mask = key_mask[0]

    def grid_spec(grid, in_specs, out_specs, scratch=()):
        return pltpu.PrefetchScalarGridSpec(
            num_scalar_prefetch=1, grid=grid, in_specs=in_specs, out_specs=out_specs, scratch_shapes=list(scratch)
        )

    slot = lambda at: once((None, size, width), lambda *_: (at, 0, 0))
    all_rows = whole(total, width)
    vectors = whole(8, width)
    own_q, own_k, own_v, own_mb = pl.pallas_call(
        project_own,
        grid_spec=grid_spec(
            (3,),
            [slot(0), whole(1, size), pl.BlockSpec((width, width), lambda i, m: (0, i)), vectors],
            [whole(width, size), whole(size, width), whole(width, size), whole(size, 128)],
        ),
        out_shape=[sds((width, size), BF), sds((size, width), BF), sds((width, size), BF), sds((size, 128), F32)],
        compiler_params=params(60),
        cost_estimate=cost(1e9, 1),
        name="project_own",
    )(meta, tok, own_mask[0:1], w_qkv, vec)
    other_mask = flip(after(own_mask, own_mb), "blk", 1)
    masks = jnp.stack([jnp.where(side == 0, own_mask[1], other_mask[1]), other_mask[0]])
    cot = cotangent[0]
    cot_came = lax.ppermute(after(cot[1, half_rows:], came), "blk", [(0, 1)])

    pair_q = pl.BlockSpec((128, total), lambda p, m: (p, 0))
    pair_rows = pl.BlockSpec((3, size, 128), lambda p, m: (0, 0, p))
    pair_cols = pl.BlockSpec((3, 128, size), lambda p, m: (0, p, 0))
    pair_probs = pl.BlockSpec((2, size, total), lambda p, m: (p, 0, 0))
    pair_inv = pl.BlockSpec((1, 2, total), lambda p, m: (p, 0, 0))
    probs, att, att_t, inv, q_t, k, v_t, tok_two = pl.pallas_call(
        functools.partial(attention_forward, heads),
        grid_spec=grid_spec(
            (pairs,),
            [whole(2, size), vectors] + [anywhere] * 7,
            [pair_probs, pl.BlockSpec((total, 128), lambda p, m: (0, p)), pair_q, pair_inv] + [anywhere] * 4,
            [
                pltpu.VMEM((width, total), BF), pltpu.VMEM((3, size, width), BF), pltpu.VMEM((3, width, size), BF),
                pltpu.VMEM((3, size, 128), F32), pltpu.VMEM((width, 3 * width), BF), pltpu.VMEM((size, width), BF),
                pltpu.VMEM((size, width), BF), pltpu.SemaphoreType.DMA((9,)), pltpu.SemaphoreType.DMA((4,)),
            ],
        ),
        out_shape=[
            sds((heads, size, total), BF), sds((total, width), BF), sds((width, total), BF),
            sds((pairs, 2, total), F32), sds((width, total), BF), sds((3, size, width), BF), sds((3, width, size), BF),
            sds((size, width), BF),
        ],
        compiler_params=params(60),
        cost_estimate=cost(1e11, 1),
        name="attention_forward",
    )(meta, masks, vec, tok, came, w_qkv, own_q, own_k, own_v, own_mb)

    chunk = 1024
    steps = hidden // chunk
    back_steps = 4
    half = owners // 2
    back_rows = hidden // owners
    back_half = pl.BlockSpec((half // back_steps, back_rows, width), lambda i, m: (jnp.maximum(i - steps, 0), 0, 0))
    flat = lambda dtype, columns=width: sds((total, columns), dtype)
    early = lambda i: jnp.minimum(i, steps - 1)
    side_rows = once((half_rows, width), lambda i, m: (m[SIDE], 0))
    slope, back_keep, back_send, sums_two, first, normed_low, mixed, mixed_two, g_second, back_low = pl.pallas_call(
        functools.partial(rows_forward, steps),
        grid_spec=grid_spec(
            (steps + back_steps,),
            [
                slot(0), side_rows, all_rows, slot(0), once((None, half_rows, width), lambda i, m: (1, 0, 0)),
                whole(half_rows, width), whole(width, width), vectors,
                pl.BlockSpec((width, chunk), lambda i, m: (0, early(i))),
                pl.BlockSpec((1, chunk), lambda i, m: (0, early(i))),
                pl.BlockSpec((chunk, width), lambda i, m: (early(i), 0)),
            ],
            [
                pl.BlockSpec((total, chunk), lambda i, m: (0, early(i))),
                back_half, back_half, whole(8, width),
            ]
            + [anywhere] * 6,
            [
                pltpu.VMEM((total, width), F32), pltpu.VMEM((total, width), BF), pltpu.VMEM((total, width), BF),
                pltpu.VMEM((total, width), F32), pltpu.VMEM((total, width), BF), pltpu.VMEM((total, hidden), BF),
                pltpu.SemaphoreType.DMA((6,)),
            ],
        ),
        out_shape=[
            flat(BF, hidden), sds((half, back_rows, width), BF), sds((half, back_rows, width), BF),
            sds((8, width), F32), flat(F32), flat(BF),
            sds((size, width), BF), sds((half_rows, width), BF), flat(F32), flat(BF),
        ],
        compiler_params=params(60),
        cost_estimate=cost(1e11, 1),
        name="rows_forward",
    )(
        meta, tok, tok_two, att, cot, cot, cot_came, w_out, vec, w_in, bias_in.reshape(1, hidden), w_back,
    )

    back = Piece(back_keep, [back_send], True)
    take(meta, [back])
    back_low = after(back_low, back.sending)
    mixed_came = lax.ppermute(mixed_two, "blk", [(1, 0)])

    own_rows = width // owners
    in_steps = hidden // width
    in_early = lambda i: jnp.minimum(i, in_steps - 1)
    in_half = pl.BlockSpec((half, own_rows, width), lambda i, m: (0, 0, i))
    in_keep, *rest = pl.pallas_call(
        rows_backward,
        grid_spec=grid_spec(
            (in_steps + 1,),
            [
                all_rows, all_rows, pl.BlockSpec((total, width), lambda i, m: (0, in_early(i))),
                pl.BlockSpec((width, width), lambda i, m: (0, in_early(i))),
                pl.BlockSpec((width, width), lambda i, m: (in_early(i), 0)),
                whole(width, width), vectors, anywhere, anywhere, anywhere,
            ],
            [
                in_half, *[whole(half, own_rows, width)] * (in_steps + 1), all_rows, all_rows, whole(width, total),
                pl.BlockSpec((1, width), lambda i, m: (0, in_early(i))), whole(8, width),
            ],
            [
                pltpu.VMEM((total, width), F32), pltpu.VMEM((total, width), F32), pltpu.VMEM((total, width), F32),
                pltpu.VMEM((width, total), BF), pltpu.SemaphoreType.DMA((3,)),
            ],
        ),
        out_shape=[
            sds((half, own_rows, hidden + width), BF), *[sds((half, own_rows, width), BF)] * (in_steps + 1), flat(F32),
            flat(BF),
            sds((width, total), BF), sds((1, hidden), F32), sds((8, width), F32),
        ],
        compiler_params=params(60),
        cost_estimate=cost(1e11, 1),
        name="rows_backward",
    )(meta, back_low, normed_low, slope, w_in, w_back, w_out, vec, first, g_second, att_t)
    in_sends, (g_first, first_low, do_t, g_b_in, sums_one) = rest[:-5], rest[-5:]
    inner = Piece(in_keep, in_sends, False)
    do_t = after(do_t, *take(meta, [back], do_t))
    do_t = after(do_t, *take(meta, [inner], do_t))
    gq_shapes = [
        sds((width, total), BF), sds((3, 2, width, size), BF), sds((1, width), F32), sds((1, width), F32),
    ]

    gq_t, gkv_t, g_bq, g_bv = pl.pallas_call(
        functools.partial(attention_backward, heads),
        grid_spec=grid_spec(
            (pairs,),
            [pair_probs, pair_rows, pair_cols, pair_q, pair_q, pair_q, pair_inv],
            [pair_q, pl.BlockSpec((3, 2, 128, size), lambda p, m: (0, 0, p, 0))]
            + [pl.BlockSpec((1, 128), lambda p, m: (0, p))] * 2,
            [
                pltpu.VMEM((3, 128, size), F32), pltpu.VMEM((3, 128, size), F32), pltpu.VMEM((128, total), F32),
                pltpu.VMEM((3, 128, size), BF), pltpu.VMEM((3, size, 128), BF),
            ],
        ),
        out_shape=gq_shapes,
        compiler_params=params(60),
        cost_estimate=cost(1e11, 1),
        name="attention_backward",
    )(meta, probs, k, v_t, q_t, do_t, att_t, inv)
    gkv_t = gkv_t.reshape(3, 2 * width, size)
    gq_t = after(gq_t, mixed_came, *take(meta, [back], gq_t))

    columns = 3 * width + 128
    vmem = pl.BlockSpec(memory_space=pltpu.VMEM)
    run_weights = pl.pallas_call(
        weight_gradients,
        in_specs=[pl.BlockSpec(memory_space=pltpu.SMEM)] + [anywhere] * 5 + [vmem] * 5,
        out_specs=[anywhere] * 2,
        scratch_shapes=[
            pltpu.VMEM((3, size, width), BF), pltpu.VMEM((width, total), BF), pltpu.VMEM((3, 2 * width, size), BF),
            pltpu.VMEM((width, 3 * size), BF),
            pltpu.VMEM((2, half, own_rows, width), BF), pltpu.VMEM((2, half, own_rows, width), BF),
            pltpu.VMEM((half, own_rows, 128), BF), pltpu.VMEM((half, own_rows, 128), BF),
            pltpu.SemaphoreType.DMA((7,)), pltpu.SemaphoreType.DMA((6,)),
        ],
        out_shape=[sds((half, own_rows, columns), BF)] * 2,
        compiler_params=params(60),
        cost_estimate=cost(4e9, 1),
        name="weight_gradients",
    )
    last_keep, last_send = run_weights(
        meta, tok, tok_two, came, gq_t, gkv_t, sums_two, sums_one, g_bq, g_bv, g_b_in
    )
    last = Piece(last_keep, [last_send], False)
    shown = take(meta, [inner, back], last_keep)
    gq_t = after(gq_t, *shown, inner.sending, back.sending)

    sent, two_own, own_grad = pl.pallas_call(
        tokens_backward,
        grid_spec=grid_spec(
            (3,),
            [
                whole(width, 3 * width), whole(width, total),
                pl.BlockSpec((None, 2 * width, size), lambda i, m: (2 - i, 0, 0)), all_rows,
            ],
            [whole(2, size, width), whole(size, width), whole(size, width)],
            [pltpu.VMEM((width, 2 * width), BF), pltpu.VMEM((width, width), BF)],
        ),
        out_shape=[sds((2, size, width), BF), sds((size, width), F32), sds((size, width), F32)],
        compiler_params=params(60),
        cost_estimate=cost(1e11, 1),
        name="tokens_backward",
    )(meta, w_qkv, gq_t, gkv_t, g_first)
    came_grad = flip(sent, "blk", 1)
    shown = take(meta, [last], own_grad)
    shown = take(meta, [last, inner], last.sending)
    while last.stage is not None:
        shown = take(meta, [piece for piece in (last, inner, back) if piece.stage is not None], *shown)

    out_back = back.finish(side)
    out_in = inner.finish(side)
    out_last = last.finish(side)

    came_grad = after(came_grad, *shown).astype(F32)
    tokens_grad = jnp.stack([own_grad + came_grad[0], jnp.where(side == 0, two_own + came_grad[1], 0.0)]).astype(BF)[None]
    mixed_other = jnp.where(side == 0, jnp.concatenate([mixed_two, mixed_came]), jnp.zeros((), BF))
    mixed_all = jnp.stack([mixed, mixed_other])[None]
    pick = lambda at: out_last[:, 3 * width + at]
    line = min(64, back_rows)
    return (
        mixed_all, tokens_grad,
        out_last[:, : 3 * width], pick(6), pick(7), out_in[:, hidden:], pick(5), pick(3), pick(4),
        out_in[:, :hidden], out_last[: back_rows // line, 3 * width + 64 : 3 * width + 64 + line].reshape(-1), out_back, pick(2), pick(0),
        pick(1),
    )


def solution(mesh):
    split = P("batch", None, "blk", None)
    in_specs = (split, split, P("batch"), P(), P("batch", None, "blk")) + (P(),) * 13
    matrix, vector = P("batch", None), P("batch")
    out_specs = (
        split, split, matrix, vector, vector, matrix, vector, vector, vector, matrix, vector, matrix, vector, vector,
        vector,
    )
    return jax.shard_map(local, mesh=mesh, in_specs=in_specs, out_specs=out_specs, check_vma=False)
```

time: 341 us -> 263 us (0.77)
  Pallas kernels: 165 us -> 124 us
  waiting for transfers between devices: 89.7 us -> 64.2 us
  other arithmetic: 14.3 us -> 8.45 us
  starting transfers between devices: 41 us -> 36.5 us
    pallas_call x16 -> x12, Pallas kernels: 108 us -> 64.4 us  [the longest x1 24.1 us: local(): pl.pallas_call(rows_backward, grid_spec=grid_spec((in_steps + 1,), [all_r...]
    ppermute x4 -> x2, waiting for transfers between devices: 31.6 us -> 0.01 us  [the longest x1 0.01 us: local(): cot_came = lax.ppermute(after(cot[1, half_rows:], came), 'blk', [(0, 1)])]
    ppermute x30 -> x17, starting transfers between devices: 31.6 us -> 17.7 us  [flip(): return lax.ppermute(value, axis, [(at, at ^ bit) for at in range(count)])]
    all_to_all x0 -> x3, starting transfers between devices: none -> 13.3 us  [the longest x2 9.71 us: taken(): came = lax.all_to_all(results[0], 'batch', 0, 0, axis_index_groups=groups)]
    pallas_call x1, Pallas kernels: 12.1 us -> 19.7 us  [local(): pl.pallas_call(functools.partial(attention_forward, heads), grid_spec=gri...]
    all_to_all x0 -> x3, waiting for transfers between devices: none -> 6.63 us  [the longest x2 3.75 us: taken(): came = lax.all_to_all(results[0], 'batch', 0, 0, axis_index_groups=groups)]
    pallas_call x1, Pallas kernels: 30.4 us -> 24.2 us  [local(): pl.pallas_call(functools.partial(rows_forward, steps), grid_spec=grid_spe...]
    unnamed x77 -> x56, local copies, waits for them, and re-layouts: 10.4 us -> 16.5 us
  transfers between devices with their start and end apart: 34 -> 22, of which waited for: 12 -> 10; matrix products, arithmetic and copies ran while one was open for 9% -> 7% of each run, Pallas kernels for 32% -> 37%
where the time goes in v2:
time: 263 us; the launch traced here: 259 us
  Pallas kernels  124 us (47%)
  waiting for transfers between devices  64.2 us (24%)
  starting transfers between devices  36.5 us (14%)
  local copies, waits for them, and re-layouts  24.6 us (9%)
  other arithmetic  8.45 us (3%)
    ppermute x17, waiting for transfers between devices, flip(): return lax.ppermute(value, axis, [(at, at ^ bit) for at in range(count)])  57.5 us
    pallas_call x1, Pallas kernels, local(): pl.pallas_call(functools.partial(rows_forward, steps), grid_spec=grid_spe...  24.2 us
    pallas_call x1, Pallas kernels, local(): pl.pallas_call(rows_backward, grid_spec=grid_spec((in_steps + 1,), [all_r...  24.1 us
    pallas_call x1, Pallas kernels, local(): pl.pallas_call(functools.partial(attention_forward, heads), grid_spec=gri...  19.7 us
    ppermute x17, starting transfers between devices, flip(): return lax.ppermute(value, axis, [(at, at ^ bit) for at in range(count)])  17.7 us
    unnamed x56, local copies, waits for them, and re-layouts  16.5 us
    pallas_call x1, Pallas kernels, local(): pl.pallas_call(functools.partial(attention_backward, heads), grid_spec=gr...  15.3 us
    pallas_call x1, Pallas kernels, local(): pl.pallas_call(tokens_backward, grid_spec=grid_spec((3,), [whole(width, 3...  12.5 us
  transfers between devices with their start and end apart: 22, of which 10 were waited for; matrix products, arithmetic and copies ran while one was open for 7% of the time, Pallas kernels for 37%

profile of v2, /device:TPU:0, one launch (start us, length us, event | category | flops | bytes accessed | tf_op | source)
XLA Modules:
  0.0 259.3 jit_solution(1447679822243253643)
XLA Ops:
  0.6 3.0 %collective-permute-start.1 = (bf16[2,512,768]{2,1,0:T(8,128)(2,1)}, bf16[2,512,768]{2,1,0:T(8,128)(2,1)S(1)}, u32[]{:S(2)}, u32[]{:S(2)}) collective-permute-start(bf16[2,512,768]{2,1,0:T(8,128)(2,1)} %bitcast.54), channel_id=1, source_target_pairs={{0,1},{1,0},{2,3},{3,2},{4,5},{5,4},{6,7},{7,6},{8,9},{9,8},{10,11... | collective-permute-start | bytes 4718600 | tf_op jit(solution)/shard_map/ppermute | solution.py:511
  11.9 1.3 slice_bitcast_fusion.3.mask
  13.2 7.0 %project_own.1 = (bf16[768,512]{1,0:T(8,128)(2,1)}, bf16[512,768]{1,0:T(8,128)(2,1)}, bf16[768,512]{1,0:T(8,128)(2,1)}, f32[512,128]{1,0:T(8,128)}) custom-call(s32[29]{0:T(128)} %concatenate.35.meta, bf16[2,512,768]{2,1,0:T(8,128)(2,1)} %bitcast.55, s32[1,512]{1,0:T(1,128)} %slice_bitcast_fusion.3.mask, bf16[768,2304]{1,0:T(8,128)(2,1)} %w.3, ...), custom_call_target="tpu_custom_call" | custom-call | flops 1000000000 | bytes 1 | tf_op jit(solution)/shard_map/project_own/pallas_call | solution.py:680
  20.2 1.0 slice_bitcast_fusion.2
  21.2 17.2 %collective-permute-done = s32[2,512]{1,0:T(2,128)S(1)} collective-permute-done((s32[2,512]{1,0:T(2,128)S(1)}, s32[2,512]{1,0:T(2,128)S(1)}, u32[]{:S(2)}, u32[]{:S(2)}) %collective-permute-start) | collective-permute-done | bytes 4128 | tf_op jit(solution)/shard_map/ppermute | solution.py:511
  39.0 4.2 %collective-permute-start.2 = (bf16[256,768]{1,0:T(8,128)(2,1)S(1)}, bf16[256,768]{1,0:T(8,128)(2,1)S(1)}, u32[]{:S(2)}, u32[]{:S(2)}) collective-permute-start(bf16[256,768]{1,0:T(8,128)(2,1)S(1)} %slice_bitcast_fusion.2), channel_id=1, source_target_pairs={{0,1},{2,3},{4,5},{6,7},{8,9},{10,11},{12,13},{14,15},{16,17},{18,... | collective-permute-start | bytes 1179656 | tf_op jit(solution)/shard_map/ppermute | solution.py:695
  43.2 19.7 %attention_forward.1 = (bf16[12,512,768]{2,1,0:T(8,128)(2,1)}, bf16[768,768]{1,0:T(8,128)(2,1)}, bf16[768,768]{1,0:T(8,128)(2,1)}, f32[6,2,768]{2,1,0:T(2,128)},...) custom-call(s32[29]{0:T(128)} %concatenate.35.meta, ...), custom_call_target="tpu_custom_call" | custom-call | flops 99999997952 | bytes 1 | tf_op jit(solution)/shard_map/attention_forward/pallas_call | solution.py:702
  63.6 24.2 %rows_forward.1 = (bf16[768,3072]{1,0:T(8,128)(2,1)}, bf16[8,192,768]{2,1,0:T(8,128)(2,1)}, bf16[8,192,768]{2,1,0:T(8,128)(2,1)}, f32[8,768]{1,0:T(8,128)}, f32[...) custom-call(s32[29]{0:T(128)} %concatenate.35.meta, ...), custom_call_target="tpu_custom_call" | custom-call | flops 99999997952 | bytes 1 | tf_op jit(solution)/shard_map/rows_forward/pallas_call | solution.py:733
  87.9 4.7 %collective-permute-done.4.refs_1_ = bf16[8,192,768]{2,1,0:T(8,128)(2,1)S(1)} collective-permute-done((bf16[8,192,768]{2,1,0:T(8,128)(2,1)}, bf16[8,192,768]{2,1,0:T(8,128)(2,1)S(1)}, u32[]{:S(2)}, u32[]{:S(2)}) %collective-permute-start.4) | collective-permute-done | bytes 2359328 | tf_op jit(solution)/shard_map/ppermute | solution.py:511
  92.7 1.7 copy-done.3
  94.3 2.5 combine.8
  96.8 3.6 %all-to-all-start = ((bf16[4,4,192,384]{3,2,1,0:T(8,128)(2,1)}), bf16[4,4,192,384]{3,2,1,0:T(8,128)(2,1)S(1)}, u32[]{:S(2)}, u32[]{:S(2)}) async-start(bf16[4,4,192,384]{3,2,1,0:T(8,128)(2,1)} %combine.8), calls=%async_computation | async-start | bytes 4718592 | tf_op jit(solution)/shard_map/all_to_all | solution.py:594
  100.5 24.1 %rows_backward.1 = (bf16[8,48,3840]{2,1,0:T(8,128)(2,1)}, bf16[8,48,768]{2,1,0:T(8,128)(2,1)}, bf16[8,48,768]{2,1,0:T(8,128)(2,1)}, bf16[8,48,768]{2,1,0:T(8,128...) custom-call(s32[29]{0:T(128)} %concatenate.35.meta, ...), custom_call_target="tpu_custom_call" | custom-call | flops 99999997952 | bytes 1 | tf_op jit(solution)/shard_map/rows_backward/pallas_call | solution.py:776
  125.8 2.9 %all-to-all-done.refs_0_ = bf16[4,4,192,384]{3,2,1,0:T(8,128)(2,1)S(1)} async-done(((bf16[4,4,192,384]{3,2,1,0:T(8,128)(2,1)}), bf16[4,4,192,384]{3,2,1,0:T(8,128)(2,1)S(1)}, u32[]{:S(2)}, u32[]{:S(2)}) %all-to-all-start) | async-done | bytes 2359328 | tf_op jit(solution)/shard_map/all_to_all | solution.py:594
  128.7 1.4 combine.9
  130.8 1.3 collective-permute-start.3
  132.1 1.6 collective-permute-start.5
  133.8 1.8 copy-done.2
  135.6 2.1 combine.11
  137.7 1.5 copy-done
  139.3 3.9 %all-to-all-start.1 = ((bf16[4,2,48,3840]{3,2,1,0:T(8,128)(2,1)}), bf16[4,2,48,3840]{3,2,1,0:T(8,128)(2,1)S(1)}, u32[]{:S(2)}, u32[]{:S(2)}) async-start(bf16[4,2,48,3840]{3,2,1,0:T(8,128)(2,1)} %copy-done), calls=%async_computation.1 | async-start | bytes 5898240 | tf_op jit(solution)/shard_map/all_to_all | solution.py:599
  143.2 15.3 %attention_backward.1 = (bf16[768,768]{1,0:T(8,128)(2,1)}, bf16[3,2,768,512]{3,2,1,0:T(8,128)(2,1)}, f32[1,768]{1,0:T(1,128)}, f32[1,768]{1,0:T(1,128)}) custom-call(s32[29]{0:T(128)} %concatenate.35.meta, bf16[12,512,768]{2,1,0:T(8,128)(2,1)} %get-tuple-element.104.probs, bf16[3,512,768]{2,1,0:T(8,128)(2,1)} %get-tuple-element.105.k, ...), custom_call_target="tpu_custom_call" | custom-call | flops 99999997952 | bytes 1 | tf_op jit(solution)/shard_map/attention_backward/pallas_call | solution.py:812
  158.5 1.1 combine.10
  160.3 2.6 %collective-permute-start.11 = (bf16[1,192,384]{2,1,0:T(8,128)(2,1)S(1)}, bf16[1,192,384]{2,1,0:T(8,128)(2,1)S(1)}, u32[]{:S(2)}, u32[]{:S(2)}) collective-permute-start(bf16[1,192,384]{2,1,0:T(8,128)(2,1)S(1)} %get-tuple-element.150), channel_id=1, source_target_pairs={{0,16},{2,18},{4,20},{6,22},{8,24},{10,26},{12,28},{14,30},{16,0},... | collective-permute-start | bytes 442376 | tf_op jit(solution)/shard_map/ppermute | solution.py:511
  162.9 9.5 %weight_gradients.1 = (bf16[8,48,2432]{2,1,0:T(8,128)(2,1)}, bf16[8,48,2432]{2,1,0:T(8,128)(2,1)}) custom-call(s32[29]{0:T(128)} %concatenate.35.meta, bf16[2,512,768]{2,1,0:T(8,128)(2,1)} %bitcast.58, bf16[512,768]{1,0:T(8,128)(2,1)} %get-tuple-element.99.two_half.two_in, bf16[2,512,768]{2,1,0:T(8,128)(2,1)} %copy-done.22, ...), custom_call_target="tpu_custom_call" | custom-call | flops 4000000000 | bytes 1 | tf_op jit(solution)/shard_map/weight_gradients/pallas_call | solution.py:850
  172.4 5.2 %collective-permute-done.11.refs_2_ = bf16[1,192,384]{2,1,0:T(8,128)(2,1)S(1)} collective-permute-done((bf16[1,192,384]{2,1,0:T(8,128)(2,1)S(1)}, bf16[1,192,384]{2,1,0:T(8,128)(2,1)S(1)}, u32[]{:S(2)}, u32[]{:S(2)}) %collective-permute-start.11) | collective-permute-done | bytes 147488 | tf_op jit(solution)/shard_map/ppermute | solution.py:511
  178.2 1.5 all-to-all-done.1.refs_0_
  179.7 0.9 copy-done.8
  180.7 0.9 copy-done.10
  181.6 0.9 combine.12
  183.3 12.5 %tokens_backward.1 = (bf16[2,512,768]{2,1,0:T(8,128)(2,1)}, f32[512,768]{1,0:T(8,128)}, f32[512,768]{1,0:T(8,128)}) custom-call(s32[29]{0:T(128)} %concatenate.35.meta, bf16[768,2304]{1,0:T(8,128)(2,1)} %w.3, bf16[768,768]{1,0:T(8,128)(2,1)} %get-tuple-element.156.gq_in.gq_t, bf16[3,1536,512]{2,1,0:T(8,128)(2,1)} %bitcast.67, ...), custom_call_target="tpu_custom_call" | custom-call | flops 99999997952 | bytes 1 | tf_op jit(solution)/shard_map/tokens_backward/pallas_call | solution.py:857
  195.8 1.9 combine.13
  197.7 1.3 copy-done.1
  199.0 5.8 %all-to-all-start.2 = ((bf16[4,2,48,2432]{3,2,1,0:T(8,128)(2,1)}), bf16[4,2,48,2432]{3,2,1,0:T(8,128)(2,1)S(1)}, u32[]{:S(2)}, u32[]{:S(2)}) async-start(bf16[4,2,48,2432]{3,2,1,0:T(8,128)(2,1)} %copy-done.1), calls=%async_computation.2 | async-start | bytes 3735552 | tf_op jit(solution)/shard_map/all_to_all | solution.py:599
  204.8 3.1 %collective-permute-start.12 = (bf16[2,512,768]{2,1,0:T(8,128)(2,1)}, bf16[2,512,768]{2,1,0:T(8,128)(2,1)}, u32[]{:S(2)}, u32[]{:S(2)}) collective-permute-start(bf16[2,512,768]{2,1,0:T(8,128)(2,1)} %get-tuple-element.159), channel_id=1, source_target_pairs={{0,1},{1,0},{2,3},{3,2},{4,5},{5,4},{6,7},{7,6},{8,9},{9,8},{10,11... | collective-permute-start | bytes 4718600 | tf_op jit(solution)/shard_map/ppermute | solution.py:511
  208.0 1.2 maximum_select_fusion
  209.4 1.3 maximum_bitcast_fusion
  210.7 20.2 %collective-permute-done.14.refs_2_ = bf16[1,48,3840]{2,1,0:T(8,128)(2,1)S(1)} collective-permute-done((bf16[1,48,3840]{2,1,0:T(8,128)(2,1)S(1)}, bf16[1,48,3840]{2,1,0:T(8,128)(2,1)S(1)}, u32[]{:S(2)}, u32[]{:S(2)}) %collective-permute-start.14) | collective-permute-done | bytes 368672 | tf_op jit(solution)/shard_map/ppermute | solution.py:511
  230.9 2.2 all-to-all-done.2.refs_0_
  233.2 0.9 combine.14
  234.0 1.2 collective-permute-start.15
  235.2 7.9 %collective-permute-done.18 = bf16[192,384]{1,0:T(8,128)(2,1)S(1)} collective-permute-done((bf16[192,384]{1,0:T(8,128)(2,1)S(1)}, bf16[192,384]{1,0:T(8,128)(2,1)S(1)}, u32[]{:S(2)}, u32[]{:S(2)}) %collective-permute-start.18) | collective-permute-done | bytes 147488 | tf_op jit(solution)/shard_map/ppermute | solution.py:511
  243.2 0.9 maximum_convert_fusion
  244.1 1.7 collective-permute-start.17
  246.4 2.8 %collective-permute-start.16 = (bf16[48,2432]{1,0:T(8,128)(2,1)S(1)}, bf16[48,2432]{1,0:T(8,128)(2,1)S(1)}, u32[]{:S(2)}, u32[]{:S(2)}) collective-permute-start(bf16[48,2432]{1,0:T(8,128)(2,1)S(1)} %combine.15), channel_id=1, source_target_pairs={{0,1},{1,0},{2,3},{3,2},{4,5},{5,4},{6,7},{7,6},{8,9},{9,8},{10,11... | collective-permute-start | bytes 700424 | tf_op jit(solution)/shard_map/ppermute | solution.py:511
  249.2 1.6 convert_element_type.28
  251.4 1.3 pad_maximum_fusion
  254.8 1.8 collective-permute-done.16
  (93 shorter events, 19.1 us)
Async XLA Ops:
  0.6 38.3 %collective-permute-start.1 = (bf16[2,512,768]{2,1,0:T(8,128)(2,1)}, bf16[2,512,768]{2,1,0:T(8,128)(2,1)S(1)}, u32[]{:S(2)}, u32[]{:S(2)}) collective-permute-start(bf16[2,512,768]{2,1,0:T(8,128)(2,1)} %bitcast.54), channel_id=1, source_target_pairs={{0,1},{1,0},{2,3},{3,2},{4,5},{5,4},{6,7},{7,6},{8,9},{9,8},{10,11... | collective-permute-start | bytes 4718600 | tf_op jit(solution)/shard_map/ppermute | solution.py:511
  13.2 7.0 %copy-start.21 = (s32[1,2,512]{2,1,0:T(2,128)S(1)}, s32[1,2,512]{2,1,0:T(2,128)}, u32[]{:S(2)}) copy-start(s32[1,2,512]{2,1,0:T(2,128)} %param.22) | copy-start | bytes 12292
  20.1 18.2 %collective-permute-start = (s32[2,512]{1,0:T(2,128)S(1)}, s32[2,512]{1,0:T(2,128)S(1)}, u32[]{:S(2)}, u32[]{:S(2)}) collective-permute-start(s32[2,512]{1,0:T(2,128)S(1)} %bitcast.64), channel_id=1, source_target_pairs={{0,1},{1,0},{2,3},{3,2},{4,5},{5,4},{6,7},{7,6},{8,9},{9,8},{10,11... | collective-permute-start | bytes 12296 | tf_op jit(solution)/shard_map/ppermute | solution.py:511
  39.0 4.2 %copy-start.22 = (bf16[2,512,768]{2,1,0:T(8,128)(2,1)}, bf16[2,512,768]{2,1,0:T(8,128)(2,1)S(1)}, u32[]{:S(2)}) copy-start(bf16[2,512,768]{2,1,0:T(8,128)(2,1)S(1)} %collective-permute-done.1.came_in.other_in) | copy-start | bytes 4718596
  39.0 23.9 %collective-permute-start.2 = (bf16[256,768]{1,0:T(8,128)(2,1)S(1)}, bf16[256,768]{1,0:T(8,128)(2,1)S(1)}, u32[]{:S(2)}, u32[]{:S(2)}) collective-permute-start(bf16[256,768]{1,0:T(8,128)(2,1)S(1)} %slice_bitcast_fusion.2), channel_id=1, source_target_pairs={{0,1},{2,3},{4,5},{6,7},{8,9},{10,11},{12,13},{14,15},{16,17},{18,... | collective-permute-start | bytes 1179656 | tf_op jit(solution)/shard_map/ppermute | solution.py:695
  62.9 0.7 copy-start.23
  63.6 29.0 %copy-start.11 = (s32[29]{0:T(128)S(1)}, s32[29]{0:T(128)}, u32[]{:S(2)}) copy-start(s32[29]{0:T(128)} %concatenate.35.meta) | copy-start | bytes 352
  87.8 4.8 %collective-permute-start.4 = (bf16[8,192,768]{2,1,0:T(8,128)(2,1)}, bf16[8,192,768]{2,1,0:T(8,128)(2,1)S(1)}, u32[]{:S(2)}, u32[]{:S(2)}) collective-permute-start(bf16[8,192,768]{2,1,0:T(8,128)(2,1)} %get-tuple-element.110), channel_id=1, source_target_pairs={{0,2},{2,0},{4,6},{6,4},{8,10},{10,8},{12,14},{14,12},{16,18},{18,... | collective-permute-start | bytes 7077896 | tf_op jit(solution)/shard_map/ppermute | solution.py:511
  92.7 1.7 copy-start.3
  96.8 31.9 %all-to-all-start = ((bf16[4,4,192,384]{3,2,1,0:T(8,128)(2,1)}), bf16[4,4,192,384]{3,2,1,0:T(8,128)(2,1)S(1)}, u32[]{:S(2)}, u32[]{:S(2)}) async-start(bf16[4,4,192,384]{3,2,1,0:T(8,128)(2,1)} %combine.8), calls=%async_computation | async-start | bytes 4718592 | tf_op jit(solution)/shard_map/all_to_all | solution.py:594
  100.4 28.2 %copy-start.12 = (s32[29]{0:T(128)S(1)}, s32[29]{0:T(128)}, u32[]{:S(2)}) copy-start(s32[29]{0:T(128)} %concatenate.35.meta) | copy-start | bytes 352
  124.6 6.2 %collective-permute-start.10 = (bf16[8,48,768]{2,1,0:T(8,128)(2,1)}, bf16[8,48,768]{2,1,0:T(8,128)(2,1)S(1)}, u32[]{:S(2)}, u32[]{:S(2)}) collective-permute-start(bf16[8,48,768]{2,1,0:T(8,128)(2,1)} %get-tuple-element.135), channel_id=1, source_target_pairs={{0,2},{2,0},{4,6},{6,4},{8,10},{10,8},{12,14},{14,12},{16,18},{18,... | collective-permute-start | bytes 1769480 | tf_op jit(solution)/shard_map/ppermute | solution.py:511
  124.8 7.3 %collective-permute-start.6 = (bf16[8,48,768]{2,1,0:T(8,128)(2,1)}, bf16[8,48,768]{2,1,0:T(8,128)(2,1)S(1)}, u32[]{:S(2)}, u32[]{:S(2)}) collective-permute-start(bf16[8,48,768]{2,1,0:T(8,128)(2,1)} %get-tuple-element.131), channel_id=1, source_target_pairs={{0,2},{2,0},{4,6},{6,4},{8,10},{10,8},{12,14},{14,12},{16,18},{18,... | collective-permute-start | bytes 1769480 | tf_op jit(solution)/shard_map/ppermute | solution.py:511
  125.1 8.6 %collective-permute-start.7 = (bf16[8,48,768]{2,1,0:T(8,128)(2,1)}, bf16[8,48,768]{2,1,0:T(8,128)(2,1)}, u32[]{:S(2)}, u32[]{:S(2)}) collective-permute-start(bf16[8,48,768]{2,1,0:T(8,128)(2,1)} %get-tuple-element.132), channel_id=1, source_target_pairs={{0,2},{2,0},{4,6},{6,4},{8,10},{10,8},{12,14},{14,12},{16,18},{18,... | collective-permute-start | bytes 1769480 | tf_op jit(solution)/shard_map/ppermute | solution.py:511
  125.3 8.5 %collective-permute-start.8 = (bf16[8,48,768]{2,1,0:T(8,128)(2,1)}, bf16[8,48,768]{2,1,0:T(8,128)(2,1)}, u32[]{:S(2)}, u32[]{:S(2)}) collective-permute-start(bf16[8,48,768]{2,1,0:T(8,128)(2,1)} %get-tuple-element.133), channel_id=1, source_target_pairs={{0,2},{2,0},{4,6},{6,4},{8,10},{10,8},{12,14},{14,12},{16,18},{18,... | collective-permute-start | bytes 1769480 | tf_op jit(solution)/shard_map/ppermute | solution.py:511
  125.7 8.1 %collective-permute-start.9 = (bf16[8,48,768]{2,1,0:T(8,128)(2,1)}, bf16[8,48,768]{2,1,0:T(8,128)(2,1)}, u32[]{:S(2)}, u32[]{:S(2)}) collective-permute-start(bf16[8,48,768]{2,1,0:T(8,128)(2,1)} %get-tuple-element.134), channel_id=1, source_target_pairs={{0,2},{2,0},{4,6},{6,4},{8,10},{10,8},{12,14},{14,12},{16,18},{18,... | collective-permute-start | bytes 1769480 | tf_op jit(solution)/shard_map/ppermute | solution.py:511
  130.1 0.7 copy-start.5
  130.8 29.4 %collective-permute-start.3 = (bf16[256,768]{1,0:T(8,128)(2,1)}, bf16[256,768]{1,0:T(8,128)(2,1)}, u32[]{:S(2)}, u32[]{:S(2)}) collective-permute-start(bf16[256,768]{1,0:T(8,128)(2,1)} %get-tuple-element.103), channel_id=1, source_target_pairs={{1,0},{3,2},{5,4},{7,6},{9,8},{11,10},{13,12},{15,14},{17,16},{19,... | collective-permute-start | bytes 1179656 | tf_op jit(solution)/shard_map/ppermute | solution.py:770
  132.1 26.4 %collective-permute-start.5 = (bf16[2,192,384]{2,1,0:T(8,128)(2,1)}, bf16[2,192,384]{2,1,0:T(8,128)(2,1)}, u32[]{:S(2)}, u32[]{:S(2)}) collective-permute-start(bf16[2,192,384]{2,1,0:T(8,128)(2,1)} %get-tuple-element.125), channel_id=1, source_target_pairs={{0,8},{2,10},{4,12},{6,14},{8,0},{10,2},{12,4},{14,6},{16,24},{18,... | collective-permute-start | bytes 884744 | tf_op jit(solution)/shard_map/ppermute | solution.py:511
  133.8 1.8 copy-start.2
  137.7 1.6 copy-start
  139.3 40.5 %all-to-all-start.1 = ((bf16[4,2,48,3840]{3,2,1,0:T(8,128)(2,1)}), bf16[4,2,48,3840]{3,2,1,0:T(8,128)(2,1)S(1)}, u32[]{:S(2)}, u32[]{:S(2)}) async-start(bf16[4,2,48,3840]{3,2,1,0:T(8,128)(2,1)} %copy-done), calls=%async_computation.1 | async-start | bytes 5898240 | tf_op jit(solution)/shard_map/all_to_all | solution.py:599
  143.2 15.4 %copy-start.6 = (bf16[2,192,384]{2,1,0:T(8,128)(2,1)S(1)}, bf16[2,192,384]{2,1,0:T(8,128)(2,1)}, u32[]{:S(2)}) copy-start(bf16[2,192,384]{2,1,0:T(8,128)(2,1)} %copy-done.5) | copy-start | bytes 884740
  143.2 15.4 %copy-start.13 = (s32[29]{0:T(128)S(1)}, s32[29]{0:T(128)}, u32[]{:S(2)}) copy-start(s32[29]{0:T(128)} %concatenate.35.meta) | copy-start | bytes 352
  159.6 0.7 copy-start.7
  160.3 17.3 %collective-permute-start.11 = (bf16[1,192,384]{2,1,0:T(8,128)(2,1)S(1)}, bf16[1,192,384]{2,1,0:T(8,128)(2,1)S(1)}, u32[]{:S(2)}, u32[]{:S(2)}) collective-permute-start(bf16[1,192,384]{2,1,0:T(8,128)(2,1)S(1)} %get-tuple-element.150), channel_id=1, source_target_pairs={{0,16},{2,18},{4,20},{6,22},{8,24},{10,26},{12,28},{14,30},{16,0},... | collective-permute-start | bytes 442376 | tf_op jit(solution)/shard_map/ppermute | solution.py:511
  162.9 16.9 %copy-start.14 = (s32[29]{0:T(128)S(1)}, s32[29]{0:T(128)}, u32[]{:S(2)}) copy-start(s32[29]{0:T(128)} %concatenate.35.meta) | copy-start | bytes 352
  172.3 23.4 %collective-permute-start.13 = (bf16[8,48,2432]{2,1,0:T(8,128)(2,1)}, bf16[8,48,2432]{2,1,0:T(8,128)(2,1)}, u32[]{:S(2)}, u32[]{:S(2)}) collective-permute-start(bf16[8,48,2432]{2,1,0:T(8,128)(2,1)} %get-tuple-element.160), channel_id=1, source_target_pairs={{0,2},{2,0},{4,6},{6,4},{8,10},{10,8},{12,14},{14,12},{16,18},{18,... | collective-permute-start | bytes 5603336 | tf_op jit(solution)/shard_map/ppermute | solution.py:511
  177.6 0.7 copy-start.9
  179.7 0.9 copy-start.8
  180.7 0.9 copy-start.10
  182.5 0.7 copy-start.16
  183.3 12.5 %copy-start.4 = (bf16[8,48,2432]{2,1,0:T(8,128)(2,1)S(1)}, bf16[8,48,2432]{2,1,0:T(8,128)(2,1)}, u32[]{:S(2)}) copy-start(bf16[8,48,2432]{2,1,0:T(8,128)(2,1)} %get-tuple-element.161.refs_0_) | copy-start | bytes 5603332
  183.3 12.5 %copy-start.15 = (s32[29]{0:T(128)S(1)}, s32[29]{0:T(128)}, u32[]{:S(2)}) copy-start(s32[29]{0:T(128)} %concatenate.35.meta) | copy-start | bytes 352
  197.7 1.3 copy-start.1
  199.0 9.0 %copy-start.17 = (bf16[1,48,3840]{2,1,0:T(8,128)(2,1)S(1)}, bf16[1,48,3840]{2,1,0:T(8,128)(2,1)}, u32[]{:S(2)}) copy-start(bf16[1,48,3840]{2,1,0:T(8,128)(2,1)} %copy-done.16) | copy-start | bytes 1105924
  199.0 34.2 %all-to-all-start.2 = ((bf16[4,2,48,2432]{3,2,1,0:T(8,128)(2,1)}), bf16[4,2,48,2432]{3,2,1,0:T(8,128)(2,1)S(1)}, u32[]{:S(2)}, u32[]{:S(2)}) async-start(bf16[4,2,48,2432]{3,2,1,0:T(8,128)(2,1)} %copy-done.1), calls=%async_computation.2 | async-start | bytes 3735552 | tf_op jit(solution)/shard_map/all_to_all | solution.py:599
  204.8 4.6 %copy-start.20 = (bf16[512,768]{1,0:T(8,128)(2,1)S(1)}, bf16[512,768]{1,0:T(8,128)(2,1)}, u32[]{:S(2)}) copy-start(bf16[512,768]{1,0:T(8,128)(2,1)} %get-tuple-element.102) | copy-start | bytes 2359300
  204.8 44.4 %collective-permute-start.12 = (bf16[2,512,768]{2,1,0:T(8,128)(2,1)}, bf16[2,512,768]{2,1,0:T(8,128)(2,1)}, u32[]{:S(2)}, u32[]{:S(2)}) collective-permute-start(bf16[2,512,768]{2,1,0:T(8,128)(2,1)} %get-tuple-element.159), channel_id=1, source_target_pairs={{0,1},{1,0},{2,3},{3,2},{4,5},{5,4},{6,7},{7,6},{8,9},{9,8},{10,11... | collective-permute-start | bytes 4718600 | tf_op jit(solution)/shard_map/ppermute | solution.py:511
  207.9 23.0 %collective-permute-start.14 = (bf16[1,48,3840]{2,1,0:T(8,128)(2,1)S(1)}, bf16[1,48,3840]{2,1,0:T(8,128)(2,1)S(1)}, u32[]{:S(2)}, u32[]{:S(2)}) collective-permute-start(bf16[1,48,3840]{2,1,0:T(8,128)(2,1)S(1)} %copy-done.17), channel_id=1, source_target_pairs={{0,16},{2,18},{4,20},{6,22},{8,24},{10,26},{12,28},{14,30},{16,0},... | collective-permute-start | bytes 1105928 | tf_op jit(solution)/shard_map/ppermute | solution.py:511
  209.2 33.9 %collective-permute-start.18 = (bf16[192,384]{1,0:T(8,128)(2,1)S(1)}, bf16[192,384]{1,0:T(8,128)(2,1)S(1)}, u32[]{:S(2)}, u32[]{:S(2)}) collective-permute-start(bf16[192,384]{1,0:T(8,128)(2,1)S(1)} %get-tuple-element.154), channel_id=1, source_target_pairs={{0,1},{1,0},{2,3},{3,2},{4,5},{5,4},{6,7},{7,6},{8,9},{9,8},{10,11... | collective-permute-start | bytes 442376 | tf_op jit(solution)/shard_map/ppermute | solution.py:511
  234.0 11.8 %collective-permute-start.15 = (bf16[1,48,2432]{2,1,0:T(8,128)(2,1)S(1)}, bf16[1,48,2432]{2,1,0:T(8,128)(2,1)S(1)}, u32[]{:S(2)}, u32[]{:S(2)}) collective-permute-start(bf16[1,48,2432]{2,1,0:T(8,128)(2,1)S(1)} %get-tuple-element.167), channel_id=1, source_target_pairs={{0,16},{2,18},{4,20},{6,22},{8,24},{10,26},{12,28},{14,30},{16,0},... | collective-permute-start | bytes 700424 | tf_op jit(solution)/shard_map/ppermute | solution.py:511
  244.1 9.1 %collective-permute-start.17 = (bf16[48,3840]{1,0:T(8,128)(2,1)S(1)}, bf16[48,3840]{1,0:T(8,128)(2,1)S(1)}, u32[]{:S(2)}, u32[]{:S(2)}) collective-permute-start(bf16[48,3840]{1,0:T(8,128)(2,1)S(1)} %get-tuple-element.168), channel_id=1, source_target_pairs={{0,1},{1,0},{2,3},{3,2},{4,5},{5,4},{6,7},{7,6},{8,9},{9,8},{10,11... | collective-permute-start | bytes 1105928 | tf_op jit(solution)/shard_map/ppermute | solution.py:511
  246.4 4.4 %copy-start.18 = (f32[512,768]{1,0:T(8,128)S(1)}, f32[512,768]{1,0:T(8,128)}, u32[]{:S(2)}) copy-start(f32[512,768]{1,0:T(8,128)} %get-tuple-element.172) | copy-start | bytes 4718596
  246.4 4.4 %copy-start.19 = (f32[512,768]{1,0:T(8,128)S(1)}, f32[512,768]{1,0:T(8,128)}, u32[]{:S(2)}) copy-start(f32[512,768]{1,0:T(8,128)} %get-tuple-element.158) | copy-start | bytes 4718596
  246.4 10.2 %collective-permute-start.16 = (bf16[48,2432]{1,0:T(8,128)(2,1)S(1)}, bf16[48,2432]{1,0:T(8,128)(2,1)S(1)}, u32[]{:S(2)}, u32[]{:S(2)}) collective-permute-start(bf16[48,2432]{1,0:T(8,128)(2,1)S(1)} %combine.15), channel_id=1, source_target_pairs={{0,1},{1,0},{2,3},{3,2},{4,5},{5,4},{6,7},{7,6},{8,9},{9,8},{10,11... | collective-permute-start | bytes 700424 | tf_op jit(solution)/shard_map/ppermute | solution.py:511
